TPU v7x, 128 devices: a whole 4x4x4 slice. The times are simulated.
128 devices in a mesh: slab: 32 (over x, z, core), depth: 4 (over y).
Axes of the slice: x: 4, y: 4, z: 4, core: 2. Of those that a mesh axis runs over, the one named last changes fastest.
Arguments:
- generating_displacement: float32 [3, 128, 16, 512], P(None, 'slab', 'depth'), may hold values from -0.6 to 0.6
- generating_velocity: float32 [3, 128, 16, 512], P(None, 'slab', 'depth'), may hold values from -6 to 6
- generating_memory: float32 [3, 5, 5, 5, 5, 32, 4, 128], P(None, None, None, None, None, 'slab', 'depth'), may hold values from -1.8 to 1.8
- correlation_displacement: float32 [3, 128, 16, 512], P(None, 'slab', 'depth'), may hold values from -0.6 to 0.6
- correlation_velocity: float32 [3, 128, 16, 512], P(None, 'slab', 'depth'), may hold values from -6 to 6
- correlation_memory: float32 [3, 5, 5, 5, 5, 32, 4, 128], P(None, None, None, None, None, 'slab', 'depth'), may hold values from -1.8 to 1.8
- first_lame: float32 [5, 5, 5, 32, 4, 128], P(None, None, None, 'slab', 'depth'), may hold values from 0.5 to 1.5
- shear_modulus: float32 [5, 5, 5, 32, 4, 128], P(None, None, None, 'slab', 'depth'), may hold values from 0.5 to 1
- modulus_defect: float32 [5, 5, 5, 32, 4, 128], P(None, None, None, 'slab', 'depth'), may hold values from 0.05 to 0.3
- relaxation_keep: float32 [3], replicated, may hold values from 0.5 to 0.98
- density: float32 [128, 16, 512], P('slab', 'depth'), may hold values from 0.8 to 1.6
- surface_history: float32 [64, 128, 512], P(None, 'slab', 'depth'), may hold values from -0.6 to 0.6
- node_cell: int32 [128, 512], P('slab', 'depth'), may hold values from 0 to 255
- cell_filters: float32 [256, 64], replicated, may hold values from -0.75 to 0.75
Outputs:
- generating_displacement_next: float32 [3, 128, 16, 512], P(None, 'slab', 'depth')
- generating_velocity_next: float32 [3, 128, 16, 512], P(None, 'slab', 'depth')
- generating_memory_next: float32 [3, 5, 5, 5, 5, 32, 4, 128], P(None, None, None, None, None, 'slab', 'depth')
- correlation_displacement_next: float32 [3, 128, 16, 512], P(None, 'slab', 'depth')
- correlation_velocity_next: float32 [3, 128, 16, 512], P(None, 'slab', 'depth')
- correlation_memory_next: float32 [3, 5, 5, 5, 5, 32, 4, 128], P(None, None, None, None, None, 'slab', 'depth')
Inputs may be any that keep to these rules, and one draw needn't show every extreme that they name: node_cell gives each surface node's source cell.
All inputs are finite; a program needn't handle non-finite values.
Results may differ from a plain program's by a relative error of at most 0.0001.
Values sent between devices are 32-bit elements; how exact they have to be, the bound alone decides.
A program may use at most 128 MiB of HBM per device.

v0:
```python
import jax
import jax.numpy as jnp
import numpy as np
from jax import lax
from jax.sharding import PartitionSpec as P

STEPS = 4
TAPS = 64


time_step = 0.04
highest = lax.Precision.HIGHEST


def shifted(value, axis, steps):
    count = lax.axis_size(axis)
    pairs = [(source, (source + steps) % count) for source in range(count)]
    return lax.ppermute(value, axis, pairs)


def shifted_2(block, axis, distance):
    devices = range(lax.axis_size(axis))
    route = [(i - distance, i) for i in devices if i - distance in devices]
    return lax.ppermute(block, axis, route)


def gll_tables():
    points = np.array([-1.0, -np.sqrt(3.0 / 7.0), 0.0, np.sqrt(3.0 / 7.0), 1.0])
    weights = np.array([0.1, 49.0 / 90.0, 32.0 / 45.0, 49.0 / 90.0, 0.1])
    number = points.shape[0]
    products = np.array(
        [
            np.prod(
                [points[target] - points[others] for others in range(number) if others != target]
            )
            for target in range(number)
        ]
    )
    derivative = np.zeros((number, number))
    for target in range(number):
        for source in range(number):
            if target == source:
                derivative[target, source] = np.sum(
                    [
                        1.0 / (points[target] - points[others])
                        for others in range(number)
                        if others != target
                    ]
                )
            else:
                derivative[target, source] = (
                    products[target] / products[source] / (points[target] - points[source])
                )
    return (derivative, weights)


def weight_table(weights_np):
    return weights_np[:, None, None] * weights_np[None, :, None] * weights_np[None, None, :]


def expand_axis(array, position, elements):
    return jnp.stack(
        [
            lax.slice_in_dim(
                array, offset, offset + 4 * (elements - 1) + 1, stride=4, axis=position
            )
            for offset in range(5)
        ],
        axis=0,
    )


def to_local(extended):
    count_x = (extended.shape[1] - 1) // 4
    count_y = (extended.shape[2] - 1) // 4
    count_z = (extended.shape[3] - 1) // 4
    section = expand_axis(extended, 1, count_x)
    section = expand_axis(section, 3, count_y)
    section = expand_axis(section, 5, count_z)
    return jnp.transpose(section, (3, 2, 1, 0, 4, 5, 6))


def fold_axis(local, local_axis, element_axis):
    moved = jnp.moveaxis(local, (local_axis, element_axis), (0, -1))
    rest_shape = moved.shape[1:-1]
    elements = moved.shape[-1]
    blank = jnp.zeros_like(moved[0])
    leading = jnp.stack([moved[0], moved[1], moved[2], moved[3]], axis=-1).reshape(
        rest_shape + (4 * elements,)
    )
    trailing = jnp.stack([moved[4], blank, blank, blank], axis=-1).reshape(
        rest_shape + (4 * elements,)
    )
    pad_one = jnp.zeros(rest_shape + (1,), jnp.float32)
    pad_four = jnp.zeros(rest_shape + (4,), jnp.float32)
    return jnp.concatenate([leading, pad_one], axis=-1) + jnp.concatenate(
        [pad_four, trailing[..., : 4 * elements - 3]], axis=-1
    )


def from_local(local_force):
    section = fold_axis(local_force, 3, 6)
    section = fold_axis(section, 2, 4)
    section = fold_axis(section, 1, 2)
    return jnp.transpose(section, (0, 3, 2, 1))


def element_force(
    local_disp,
    memory,
    first_lame,
    shear_modulus,
    modulus_defect,
    relaxation_keep,
    derivative,
    weight_cube,
):
    grad_x = jnp.einsum("pq,iqbcxyz->ipbcxyz", derivative, local_disp, precision=highest)
    grad_y = jnp.einsum("pq,iaqcxyz->iapcxyz", derivative, local_disp, precision=highest)
    grad_z = jnp.einsum("pq,iabqxyz->iabpxyz", derivative, local_disp, precision=highest)
    strain_xx = grad_x[0]
    strain_yy = grad_y[1]
    strain_zz = grad_z[2]
    strain_xy = 0.5 * (grad_y[0] + grad_x[1])
    strain_xz = 0.5 * (grad_z[0] + grad_x[2])
    strain_yz = 0.5 * (grad_z[1] + grad_y[2])
    volume_strain = strain_xx + strain_yy + strain_zz
    deviator = jnp.stack(
        [
            strain_xx - volume_strain / 3.0,
            strain_yy - volume_strain / 3.0,
            strain_xy,
            strain_xz,
            strain_yz,
        ]
    )
    relaxed = jnp.sum(memory, axis=0)
    double_shear = 2.0 * shear_modulus
    pressure = first_lame * volume_strain
    stress_xx = pressure + double_shear * strain_xx - relaxed[0]
    stress_yy = pressure + double_shear * strain_yy - relaxed[1]
    stress_zz = pressure + double_shear * strain_zz + relaxed[0] + relaxed[1]
    stress_xy = double_shear * strain_xy - relaxed[2]
    stress_xz = double_shear * strain_xz - relaxed[3]
    stress_yz = double_shear * strain_yz - relaxed[4]
    flux_x = weight_cube * jnp.stack([stress_xx, stress_xy, stress_xz])
    flux_y = weight_cube * jnp.stack([stress_xy, stress_yy, stress_yz])
    flux_z = weight_cube * jnp.stack([stress_xz, stress_yz, stress_zz])
    local_force = jnp.einsum("pq,ipbcxyz->iqbcxyz", derivative, flux_x, precision=highest)
    local_force = local_force + jnp.einsum(
        "pq,iapcxyz->iaqcxyz", derivative, flux_y, precision=highest
    )
    local_force = local_force + jnp.einsum(
        "pq,iabpxyz->iabqxyz", derivative, flux_z, precision=highest
    )
    retention = relaxation_keep.reshape((-1, 1, 1, 1, 1, 1, 1, 1))
    memory_next = (
        retention * memory + (1.0 - retention) * (modulus_defect * double_shear * deviator)[None]
    )
    return (local_force, memory_next)


def node_weights(length, first_index, free_top):
    global_index = first_index + jnp.arange(length, dtype=jnp.int32)
    residue = global_index % 4
    values = jnp.where(residue == 0, 0.2, jnp.where(residue == 2, 32.0 / 45.0, 49.0 / 90.0))
    if free_top:
        values = jnp.where(global_index == 0, 0.1, values)
    return values.astype(jnp.float32)


def stiffness(displacement, memory, material):
    nodes_x, nodes_y, nodes_z = displacement.shape[1:]
    plane_x = shifted(displacement[:, :1], "slab", -1)
    extended = jnp.concatenate([displacement, plane_x], axis=1)
    plane_y = shifted_2(extended[:, :, :1], "depth", -1)
    extended = jnp.concatenate([extended, plane_y], axis=2)
    extended = jnp.concatenate([extended, extended[:, :, :, :1]], axis=3)
    local_force, memory_next = element_force(to_local(extended), memory, *material)
    assembled = from_local(local_force)
    assembled = assembled[..., :nodes_z].at[..., 0].add(assembled[..., nodes_z])
    carried_y = shifted_2(assembled[:, :, nodes_y], "depth", 1)
    assembled = assembled[:, :, :nodes_y].at[:, :, 0].add(carried_y)
    carried_x = shifted(assembled[:, nodes_x], "slab", 1)
    assembled = assembled[:, :nodes_x].at[:, 0].add(carried_x)
    return (assembled, memory_next)


def cell_taps(cells, filters):
    rows_x, rows_z = cells.shape
    one_hot = (
        jnp.arange(filters.shape[0], dtype=jnp.int32)[:, None] == cells.reshape(-1)[None, :]
    ).astype(jnp.float32)
    return jnp.dot(
        filters.T, one_hot, precision=highest, preferred_element_type=jnp.float32
    ).reshape(filters.shape[1], rows_x, rows_z)


def filter_nodes(history, new_samples, cells, filters):
    window = jnp.concatenate([history, new_samples], axis=0)
    taps = cell_taps(cells, filters)
    return jnp.stack(
        [jnp.sum(taps * window[lag + 1 : lag + 1 + TAPS], axis=0) for lag in range(STEPS)]
    )


def body(
    generating_displacement,
    generating_velocity,
    generating_memory,
    correlation_displacement,
    correlation_velocity,
    correlation_memory,
    first_lame,
    shear_modulus,
    modulus_defect,
    relaxation_keep,
    density,
    surface_history,
    node_cell,
    cell_filters,
):
    derivative_np, weights_np = gll_tables()
    derivative = jnp.asarray(derivative_np, jnp.float32)
    weight_cube = jnp.asarray(weight_table(weights_np)[:, :, :, None, None, None], jnp.float32)
    material = (first_lame, shear_modulus, modulus_defect, relaxation_keep, derivative, weight_cube)
    nodes_x, nodes_y, nodes_z = density.shape
    depth_index = lax.axis_index("depth")
    nodal_mass = (
        density
        * node_weights(nodes_x, 0, False)[:, None, None]
        * node_weights(nodes_y, depth_index * nodes_y, True)[None, :, None]
        * node_weights(nodes_z, 0, False)[None, None, :]
    )
    on_top = (depth_index == 0).astype(jnp.float32)
    silent = jnp.zeros((nodes_x, nodes_z), jnp.float32)

    def update(displacement, velocity, internal, surface_force):
        external = jnp.zeros_like(displacement).at[1, :, 0, :].set(on_top * surface_force)
        velocity = velocity + time_step * (external - internal) / nodal_mass
        displacement = displacement + time_step * velocity
        return (displacement, velocity)

    def advance(displacement, velocity, memory, surface_force):
        internal, memory = stiffness(displacement, memory, material)
        displacement, velocity = update(displacement, velocity, internal, surface_force)
        return (displacement, velocity, memory)

    displacement, velocity, memory = (
        generating_displacement,
        generating_velocity,
        generating_memory,
    )
    samples = []
    for step_index in range(STEPS):
        displacement, velocity, memory = advance(displacement, velocity, memory, silent)
        samples.append(displacement[1, :, 0, :])
    generated = (displacement, velocity, memory)
    new_samples = jnp.stack(samples)
    history_all, cells_all = (
        lax.all_gather(surface_history, "depth", axis=2, tiled=True),
        lax.all_gather(node_cell, "depth", axis=1, tiled=True),
    )
    forcing = filter_nodes(history_all, new_samples, cells_all, cell_filters)
    displacement, velocity, memory = (
        correlation_displacement,
        correlation_velocity,
        correlation_memory,
    )
    for step_index in range(STEPS):
        displacement, velocity, memory = advance(
            displacement, velocity, memory, forcing[step_index]
        )
    return (generated[0], generated[1], generated[2], displacement, velocity, memory)


def solution(mesh):
    return jax.shard_map(
        body,
        mesh=mesh,
        in_specs=(
            P(None, "slab", "depth", None),
            P(None, "slab", "depth", None),
            P(None, None, None, None, None, "slab", "depth", None),
            P(None, "slab", "depth", None),
            P(None, "slab", "depth", None),
            P(None, None, None, None, None, "slab", "depth", None),
            P(None, None, None, "slab", "depth", None),
            P(None, None, None, "slab", "depth", None),
            P(None, None, None, "slab", "depth", None),
            P(),
            P("slab", "depth", None),
            P(None, "slab", "depth"),
            P("slab", "depth"),
            P(),
        ),
        out_specs=(
            P(None, "slab", "depth", None),
            P(None, "slab", "depth", None),
            P(None, None, None, None, None, "slab", "depth", None),
            P(None, "slab", "depth", None),
            P(None, "slab", "depth", None),
            P(None, None, None, None, None, "slab", "depth", None),
        ),
        check_vma=False,
    )
```

profile of v0, /device:TPU:1, one launch (start us, length us, event | category | flops | bytes accessed | tf_op | source)
XLA Modules:
  0.0 544.1 jit_solution(4575902177097422024)
XLA Ops:
  3.6 5.8 %collective-permute-start = (f32[3,1,4,512]{3,2,1,0:T(4,128)S(1)}, f32[3,1,4,512]{3,2,1,0:T(4,128)S(1)}, u32[]{:S(2)}, u32[]{:S(2)}) collective-permute-start(f32[3,1,4,512]{3,2,1,0:T(4,128)S(1)} %slice.2355), channel_id=1, source_target_pairs={{0,124},{4,0},{8,4},{12,8},{16,12},{20,16},{24,20},{28,24},{32,28}... | collective-permute-start | bytes 73736 | tf_op jit(solution)/shard_map/ppermute | solution.py:18
  15.5 12.7 %all_gather.7 = f32[64,4,512]{2,1,0:T(4,128)S(1)} all-gather(f32[64,4,128]{2,1,0:T(4,128)} %param.91), channel_id=1, replica_groups=mesh['slab'=32,'depth'=4] {'depth'}, dimensions={2}, use_global_device_ids=true | all-gather | bytes 655360 | tf_op jit(solution)/shard_map/all_gather | solution.py:261
  29.0 8.1 %all_gather.6 = s32[4,512]{1,0:T(4,128)S(1)} all-gather(s32[4,128]{1,0:T(4,128)S(1)} %copy-done.48), channel_id=1, replica_groups=mesh['slab'=32,'depth'=4] {'depth'}, dimensions={1}, use_global_device_ids=true | all-gather | bytes 10240 | tf_op jit(solution)/shard_map/all_gather | solution.py:262
  77.4 5.9 %reshape.3459 = f32[3,5,5,1,1,512]{5,4,2,1,0,3:T(1,128)S(1)} reshape(f32[3,5,5,1,1,128,4]{6,5,4,2,1,0,3:T(8,128)} %copy.11399) | data formatting | bytes 307200 | tf_op jit(solution)/shard_map/reshape | solution.py:88
  86.4 5.7 %maximum_maximum_fusion = f32[3,5,5,1,1,128,4]{6,5,4,2,1,0,3:T(8,128)} fusion(f32[3,5,5,1,1,128,1]{6,5,4,2,1,0,3:T(8,128)} %copy.11400, f32[4]{0:T(128)S(1)} %pad.421.clone, f32[4]{0:T(128)S(1)} %pad.420.clone), kind=kLoop, calls=%fused_computation | loop fusion | flops 76800 | bytes 192032 | tf_op jit(solution)/shard_map/stack | solution.py:91
  92.1 6.3 %reshape.3460 = f32[3,5,5,1,1,512]{5,4,2,1,0,3:T(1,128)} reshape(f32[3,5,5,1,1,128,4]{6,5,4,2,1,0,3:T(8,128)} %maximum_maximum_fusion) | data formatting | bytes 307200 | tf_op jit(solution)/shard_map/reshape | solution.py:91
  127.9 6.3 %reshape.3496 = f32[3,5,5,1,1,512]{5,4,2,1,0,3:T(1,128)} reshape(f32[3,5,5,1,1,128,4]{6,5,4,2,1,0,3:T(8,128)} %copy.11573) | data formatting | bytes 307200 | tf_op jit(solution)/shard_map/reshape | solution.py:88
  135.2 4.7 collective-permute-start.4
  159.8 3.9 fusion.262
  172.2 5.8 %reshape.3468 = f32[3,5,5,1,1,512]{5,4,2,1,0,3:T(1,128)S(1)} reshape(f32[3,5,5,1,1,128,4]{6,5,4,2,1,0,3:T(8,128)} %copy.11440) | data formatting | bytes 307200 | tf_op jit(solution)/shard_map/reshape | solution.py:88
  181.2 9.8 %maximum_maximum_fusion.4 = (f32[3,5,5,1,1,128,4]{6,5,4,2,1,0,3:T(8,128)}, f32[3,5,5,1,1,128,4]{6,5,4,2,1,0,3:T(8,128)}) fusion(f32[3,5,5,1,1,128,1]{6,5,4,2,1,0,3:T(8,128)} %copy.11574, f32[4]{0:T(128)S(1)} %pad.421.clone, f32[4]{0:T(128)S(1)} %pad.420.clone, f32[3,5,5,1,1,128,1]{6,5,4,2,1,0,3:T(8,128)} %copy.11441), kind=kLoop, calls=%fused_computation.4 | loop fusion | flops 153600 | bytes 384032 | tf_op jit(solution)/shard_map/stack | solution.py:91
  191.0 5.7 %reshape.3469 = f32[3,5,5,1,1,512]{5,4,2,1,0,3:T(1,128)S(1)} reshape(f32[3,5,5,1,1,128,4]{6,5,4,2,1,0,3:T(8,128)} %get-tuple-element.891) | data formatting | bytes 307200 | tf_op jit(solution)/shard_map/reshape | solution.py:91
  197.4 5.7 %reshape.3497 = f32[3,5,5,1,1,512]{5,4,2,1,0,3:T(1,128)S(1)} reshape(f32[3,5,5,1,1,128,4]{6,5,4,2,1,0,3:T(8,128)} %get-tuple-element.890) | data formatting | bytes 307200 | tf_op jit(solution)/shard_map/reshape | solution.py:91
  214.5 7.4 %collective-permute-done.7 = f32[3,4,512]{2,0,1:T(4,128)S(1)} collective-permute-done((f32[3,4,512]{2,0,1:T(4,128)S(1)}, f32[3,4,512]{2,0,1:T(4,128)S(1)}, u32[]{:S(2)}, u32[]{:S(2)}) %collective-permute-start.7) | collective-permute-done | bytes 24608 | tf_op jit(solution)/shard_map/ppermute | solution.py:18
  222.2 6.0 %collective-permute-start.8 = (f32[3,1,4,512]{3,1,2,0:T(1,128)S(1)}, f32[3,1,4,512]{3,1,2,0:T(1,128)S(1)}, u32[]{:S(2)}, u32[]{:S(2)}) collective-permute-start(f32[3,1,4,512]{3,1,2,0:T(1,128)S(1)} %slice.2934), channel_id=1, source_target_pairs={{0,124},{4,0},{8,4},{12,8},{16,12},{20,16},{24,20},{28,24},{32,28}... | collective-permute-start | bytes 73736 | tf_op jit(solution)/shard_map/ppermute | solution.py:18
  251.3 5.7 %reshape.3477 = f32[3,5,5,1,1,512]{5,4,2,1,0,3:T(1,128)S(1)} reshape(f32[3,5,5,1,1,128,4]{6,5,4,2,1,0,3:T(8,128)} %copy.11483) | data formatting | bytes 307200 | tf_op jit(solution)/shard_map/reshape | solution.py:88
  260.2 5.7 %maximum_maximum_fusion.2 = f32[3,5,5,1,1,128,4]{6,5,4,2,1,0,3:T(8,128)} fusion(f32[3,5,5,1,1,128,1]{6,5,4,2,1,0,3:T(8,128)} %copy.11484, f32[4]{0:T(128)S(1)} %pad.421.clone, f32[4]{0:T(128)S(1)} %pad.420.clone), kind=kLoop, calls=%fused_computation.2 | loop fusion | flops 76800 | bytes 192032 | tf_op jit(solution)/shard_map/stack | solution.py:91
  265.8 5.8 %reshape.3478 = f32[3,5,5,1,1,512]{5,4,2,1,0,3:T(1,128)S(1)} reshape(f32[3,5,5,1,1,128,4]{6,5,4,2,1,0,3:T(8,128)} %maximum_maximum_fusion.2) | data formatting | bytes 307200 | tf_op jit(solution)/shard_map/reshape | solution.py:91
  277.4 4.9 collective-permute-done.11
  283.4 6.0 %collective-permute-start.12 = (f32[3,1,4,512]{3,1,2,0:T(1,128)S(1)}, f32[3,1,4,512]{3,1,2,0:T(1,128)S(1)}, u32[]{:S(2)}, u32[]{:S(2)}) collective-permute-start(f32[3,1,4,512]{3,1,2,0:T(1,128)S(1)} %slice.2981), channel_id=1, source_target_pairs={{0,124},{4,0},{8,4},{12,8},{16,12},{20,16},{24,20},{28,24},{32,28}... | collective-permute-start | bytes 73736 | tf_op jit(solution)/shard_map/ppermute | solution.py:18
  292.2 3.5 collective-permute-done.13
  317.9 5.7 %reshape.3486 = f32[3,5,5,1,1,512]{5,4,2,1,0,3:T(1,128)S(1)} reshape(f32[3,5,5,1,1,128,4]{6,5,4,2,1,0,3:T(8,128)} %copy.11526) | data formatting | bytes 307200 | tf_op jit(solution)/shard_map/reshape | solution.py:88
  323.6 3.4 copy.11527
  327.0 5.7 %maximum_maximum_fusion.3 = f32[3,5,5,1,1,128,4]{6,5,4,2,1,0,3:T(8,128)} fusion(f32[3,5,5,1,1,128,1]{6,5,4,2,1,0,3:T(8,128)} %copy.11527, f32[4]{0:T(128)S(1)} %pad.421.clone, f32[4]{0:T(128)S(1)} %pad.420.clone), kind=kLoop, calls=%fused_computation.3 | loop fusion | flops 76800 | bytes 192032 | tf_op jit(solution)/shard_map/stack | solution.py:91
  332.6 5.7 %reshape.3487 = f32[3,5,5,1,1,512]{5,4,2,1,0,3:T(1,128)S(1)} reshape(f32[3,5,5,1,1,128,4]{6,5,4,2,1,0,3:T(8,128)} %maximum_maximum_fusion.3) | data formatting | bytes 307200 | tf_op jit(solution)/shard_map/reshape | solution.py:91
  339.9 3.4 collective-permute-start.14
  344.6 3.3 collective-permute-done.15
  352.5 6.0 %collective-permute-start.20 = (f32[3,1,4,512]{3,1,2,0:T(1,128)S(1)}, f32[3,1,4,512]{3,1,2,0:T(1,128)S(1)}, u32[]{:S(2)}, u32[]{:S(2)}) collective-permute-start(f32[3,1,4,512]{3,1,2,0:T(1,128)S(1)} %slice.3082), channel_id=1, source_target_pairs={{0,124},{4,0},{8,4},{12,8},{16,12},{20,16},{24,20},{28,24},{32,28}... | collective-permute-start | bytes 73736 | tf_op jit(solution)/shard_map/ppermute | solution.py:18
  360.8 4.0 collective-permute-done.21
  376.9 3.4 fusion.261
  387.7 5.8 %reshape.3505 = f32[3,5,5,1,1,512]{5,4,2,1,0,3:T(1,128)S(1)} reshape(f32[3,5,5,1,1,128,4]{6,5,4,2,1,0,3:T(8,128)} %copy.11616) | data formatting | bytes 307200 | tf_op jit(solution)/shard_map/reshape | solution.py:88
  396.7 5.7 %maximum_maximum_fusion.5 = f32[3,5,5,1,1,128,4]{6,5,4,2,1,0,3:T(8,128)} fusion(f32[3,5,5,1,1,128,1]{6,5,4,2,1,0,3:T(8,128)} %copy.11617, f32[4]{0:T(128)S(1)} %pad.421.clone, f32[4]{0:T(128)S(1)} %pad.420.clone), kind=kLoop, calls=%fused_computation.5 | loop fusion | flops 76800 | bytes 192032 | tf_op jit(solution)/shard_map/stack | solution.py:91
  402.4 5.7 %reshape.3506 = f32[3,5,5,1,1,512]{5,4,2,1,0,3:T(1,128)S(1)} reshape(f32[3,5,5,1,1,128,4]{6,5,4,2,1,0,3:T(8,128)} %maximum_maximum_fusion.5) | data formatting | bytes 307200 | tf_op jit(solution)/shard_map/reshape | solution.py:91
  409.6 3.4 collective-permute-start.22
  414.2 3.3 collective-permute-done.23
  417.9 6.0 %collective-permute-start.24 = (f32[3,1,4,512]{3,1,2,0:T(1,128)S(1)}, f32[3,1,4,512]{3,1,2,0:T(1,128)S(1)}, u32[]{:S(2)}, u32[]{:S(2)}) collective-permute-start(f32[3,1,4,512]{3,1,2,0:T(1,128)S(1)} %slice.3130), channel_id=1, source_target_pairs={{0,124},{4,0},{8,4},{12,8},{16,12},{20,16},{24,20},{28,24},{32,28}... | collective-permute-start | bytes 73736 | tf_op jit(solution)/shard_map/ppermute | solution.py:18
  426.1 4.1 collective-permute-done.25
  446.8 5.7 %reshape.3514 = f32[3,5,5,1,1,512]{5,4,2,1,0,3:T(1,128)S(1)} reshape(f32[3,5,5,1,1,128,4]{6,5,4,2,1,0,3:T(8,128)} %copy.11663) | data formatting | bytes 307200 | tf_op jit(solution)/shard_map/reshape | solution.py:88
  455.7 5.7 %maximum_maximum_fusion.6 = f32[3,5,5,1,1,128,4]{6,5,4,2,1,0,3:T(8,128)} fusion(f32[3,5,5,1,1,128,1]{6,5,4,2,1,0,3:T(8,128)} %copy.11664, f32[4]{0:T(128)S(1)} %pad.421.clone, f32[4]{0:T(128)S(1)} %pad.420.clone), kind=kLoop, calls=%fused_computation.6 | loop fusion | flops 76800 | bytes 192032 | tf_op jit(solution)/shard_map/stack | solution.py:91
  461.4 6.1 %reshape.3515 = f32[3,5,5,1,1,512]{5,4,2,1,0,3:T(1,128)S(1)} reshape(f32[3,5,5,1,1,128,4]{6,5,4,2,1,0,3:T(8,128)} %maximum_maximum_fusion.6) | data formatting | bytes 307200 | tf_op jit(solution)/shard_map/reshape | solution.py:91
  469.0 3.3 collective-permute-start.26
  477.9 5.9 %collective-permute-start.28 = (f32[3,1,4,512]{3,1,2,0:T(1,128)S(1)}, f32[3,1,4,512]{3,1,2,0:T(1,128)S(1)}, u32[]{:S(2)}, u32[]{:S(2)}) collective-permute-start(f32[3,1,4,512]{3,1,2,0:T(1,128)S(1)} %slice.3179), channel_id=1, source_target_pairs={{0,124},{4,0},{8,4},{12,8},{16,12},{20,16},{24,20},{28,24},{32,28}... | collective-permute-start | bytes 73736 | tf_op jit(solution)/shard_map/ppermute | solution.py:18
  486.0 4.1 collective-permute-done.29
  512.3 5.7 %reshape.3523 = f32[3,5,5,1,1,512]{5,4,2,1,0,3:T(1,128)S(1)} reshape(f32[3,5,5,1,1,128,4]{6,5,4,2,1,0,3:T(8,128)} %copy.11708) | data formatting | bytes 307200 | tf_op jit(solution)/shard_map/reshape | solution.py:88
  518.0 3.4 copy.11709
  521.3 5.7 %maximum_maximum_fusion.7 = f32[3,5,5,1,1,128,4]{6,5,4,2,1,0,3:T(8,128)} fusion(f32[3,5,5,1,1,128,1]{6,5,4,2,1,0,3:T(8,128)} %copy.11709, f32[4]{0:T(128)S(1)} %pad.421.clone, f32[4]{0:T(128)S(1)} %pad.420.clone), kind=kLoop, calls=%fused_computation.7 | loop fusion | flops 76800 | bytes 192032 | tf_op jit(solution)/shard_map/stack | solution.py:91
  527.0 5.7 %reshape.3524 = f32[3,5,5,1,1,512]{5,4,2,1,0,3:T(1,128)S(1)} reshape(f32[3,5,5,1,1,128,4]{6,5,4,2,1,0,3:T(8,128)} %maximum_maximum_fusion.7) | data formatting | bytes 307200 | tf_op jit(solution)/shard_map/reshape | solution.py:91
  534.3 3.4 collective-permute-start.30
  (770 shorter events, 278.4 us)
Async XLA Ops:
  0.6 37.4 %copy-start = (f32[256,64]{0,1:T(8,128)S(1)}, f32[256,64]{0,1:T(8,128)}, u32[]{:S(2)}) copy-start(f32[256,64]{0,1:T(8,128)} %param.93) | copy-start | bytes 196612
  0.6 38.3 %copy-start.24 = (f32[3,4,4,512]{3,2,1,0:T(4,128)S(1)}, f32[3,4,4,512]{3,2,1,0:T(4,128)}, u32[]{:S(2)}) copy-start(f32[3,4,4,512]{3,2,1,0:T(4,128)} %param.80) | copy-start | bytes 294916
  0.7 28.3 %copy-start.48 = (s32[4,128]{1,0:T(4,128)S(1)}, s32[4,128]{1,0:T(4,128)}, u32[]{:S(2)}) copy-start(s32[4,128]{1,0:T(4,128)} %param.92) | copy-start | bytes 6148
  0.7 38.2 %copy-start.43 = (f32[4,4,512]{2,1,0:T(4,128)S(1)}, f32[4,4,512]{2,1,0:T(4,128)}, u32[]{:S(2)}) copy-start(f32[4,4,512]{2,1,0:T(4,128)} %param.90) | copy-start | bytes 98308
  1.5 38.1 %collective-permute-start.16 = (f32[3,1,4,512]{3,2,1,0:T(4,128)S(1)}, f32[3,1,4,512]{3,2,1,0:T(4,128)S(1)}, u32[]{:S(2)}, u32[]{:S(2)}) collective-permute-start(f32[3,1,4,512]{3,2,1,0:T(4,128)S(1)} %slice.2593), channel_id=1, source_target_pairs={{0,124},{4,0},{8,4},{12,8},{16,12},{20,16},{24,20},{28,24},{32,28}... | collective-permute-start | bytes 73736 | tf_op jit(solution)/shard_map/ppermute | solution.py:18
  3.6 37.3 %collective-permute-start = (f32[3,1,4,512]{3,2,1,0:T(4,128)S(1)}, f32[3,1,4,512]{3,2,1,0:T(4,128)S(1)}, u32[]{:S(2)}, u32[]{:S(2)}) collective-permute-start(f32[3,1,4,512]{3,2,1,0:T(4,128)S(1)} %slice.2355), channel_id=1, source_target_pairs={{0,124},{4,0},{8,4},{12,8},{16,12},{20,16},{24,20},{28,24},{32,28}... | collective-permute-start | bytes 73736 | tf_op jit(solution)/shard_map/ppermute | solution.py:18
  15.5 292.0 %copy-start.46 = (f32[3]{0:T(128)}, f32[3]{0:T(128)S(1)}, u32[]{:S(2)}) copy-start(f32[3]{0:T(128)S(1)} %broadcast_subtract_fusion) | copy-start | bytes 40
  38.0 27.2 %copy-start.3 = (f32[5,5,1,1,1]{1,0,4,3,2:T(8,128)S(1)}, f32[5,5,1,1,1]{1,0,4,3,2:T(8,128)}, u32[]{:S(2)}) copy-start(f32[5,5,1,1,1]{1,0,4,3,2:T(8,128)} %constant.857) | copy-start | bytes 304
  39.6 4.6 collective-permute-start.17
  41.0 14.2 %collective-permute-start.1 = (f32[3,5,1,512]{3,2,1,0:T(1,128)S(1)}, f32[3,5,1,512]{3,2,1,0:T(1,128)S(1)}, u32[]{:S(2)}, u32[]{:S(2)}) collective-permute-start(f32[3,5,1,512]{3,2,1,0:T(1,128)S(1)} %slice.2835), channel_id=1, source_target_pairs={{1,0},{2,1},{3,2},{5,4},{6,5},{7,6},{9,8},{10,9},{11,10},{13,12},{... | collective-permute-start | bytes 92168 | tf_op jit(solution)/shard_map/ppermute | solution.py:24
  107.7 10.9 %collective-permute-start.2 = (f32[3,5,512]{2,1,0:T(8,128)S(1)}, f32[3,5,512]{2,1,0:T(8,128)S(1)}, u32[]{:S(2)}, u32[]{:S(2)}) collective-permute-start(f32[3,5,512]{2,1,0:T(8,128)S(1)} %slice_bitcast_fusion.118), channel_id=1, source_target_pairs={{0,1},{1,2},{2,3},{4,5},{5,6},{6,7},{8,9},{9,10},{10,11},{12,13},{... | collective-permute-start | bytes 92168 | tf_op jit(solution)/shard_map/ppermute | solution.py:24
  119.5 14.7 %collective-permute-start.3 = (f32[3,4,512]{2,1,0:T(4,128)S(1)}, f32[3,4,512]{2,1,0:T(4,128)S(1)}, u32[]{:S(2)}, u32[]{:S(2)}) collective-permute-start(f32[3,4,512]{2,1,0:T(4,128)S(1)} %bitcast.2185), channel_id=1, source_target_pairs={{0,4},{4,8},{8,12},{12,16},{16,20},{20,24},{24,28},{28,32},{32,36}... | collective-permute-start | bytes 73736 | tf_op jit(solution)/shard_map/ppermute | solution.py:18
  135.2 5.5 %collective-permute-start.4 = (f32[3,1,4,512]{3,1,2,0:T(1,128)S(1)}, f32[3,1,4,512]{3,1,2,0:T(1,128)S(1)}, u32[]{:S(2)}, u32[]{:S(2)}) collective-permute-start(f32[3,1,4,512]{3,1,2,0:T(1,128)S(1)} %slice.2887), channel_id=1, source_target_pairs={{0,124},{4,0},{8,4},{12,8},{16,12},{20,16},{24,20},{28,24},{32,28}... | collective-permute-start | bytes 73736 | tf_op jit(solution)/shard_map/ppermute | solution.py:18
  140.8 4.8 collective-permute-start.5
  204.0 18.0 %copy-start.18 = (f32[3,4,4,512]{3,1,2,0:T(4,128)S(1)}, f32[3,4,4,512]{3,1,2,0:T(4,128)}, u32[]{:S(2)}) copy-start(f32[3,4,4,512]{3,1,2,0:T(4,128)} %get-tuple-element.615) | copy-start | bytes 294916
  205.5 7.7 %collective-permute-start.6 = (f32[3,5,512]{2,0,1:T(4,128)S(1)}, f32[3,5,512]{2,0,1:T(4,128)S(1)}, u32[]{:S(2)}, u32[]{:S(2)}) collective-permute-start(f32[3,5,512]{2,0,1:T(4,128)S(1)} %bitcast.2161), channel_id=1, source_target_pairs={{0,1},{1,2},{2,3},{4,5},{5,6},{6,7},{8,9},{9,10},{10,11},{12,13},{... | collective-permute-start | bytes 92168 | tf_op jit(solution)/shard_map/ppermute | solution.py:24
  210.3 3.9 collective-permute-start.18
  213.3 8.6 %collective-permute-start.7 = (f32[3,4,512]{2,0,1:T(4,128)S(1)}, f32[3,4,512]{2,0,1:T(4,128)S(1)}, u32[]{:S(2)}, u32[]{:S(2)}) collective-permute-start(f32[3,4,512]{2,0,1:T(4,128)S(1)} %bitcast.2173), channel_id=1, source_target_pairs={{0,4},{4,8},{8,12},{12,16},{16,20},{20,24},{24,28},{28,32},{32,36}... | collective-permute-start | bytes 73736 | tf_op jit(solution)/shard_map/ppermute | solution.py:18
  214.4 13.8 %collective-permute-start.19 = (f32[3,4,512]{2,1,0:T(4,128)S(1)}, f32[3,4,512]{2,1,0:T(4,128)S(1)}, u32[]{:S(2)}, u32[]{:S(2)}) collective-permute-start(f32[3,4,512]{2,1,0:T(4,128)S(1)} %bitcast.2184), channel_id=1, source_target_pairs={{0,4},{4,8},{8,12},{12,16},{16,20},{20,24},{24,28},{28,32},{32,36}... | collective-permute-start | bytes 73736 | tf_op jit(solution)/shard_map/ppermute | solution.py:18
  222.1 23.2 %copy-start.20 = (f32[3,4,4,512]{3,1,2,0:T(4,128)}, f32[3,4,4,512]{3,1,2,0:T(4,128)S(1)}, u32[]{:S(2)}) copy-start(f32[3,4,4,512]{3,1,2,0:T(4,128)S(1)} %scatter-add.89) | copy-start | bytes 294916
  222.2 6.9 %collective-permute-start.8 = (f32[3,1,4,512]{3,1,2,0:T(1,128)S(1)}, f32[3,1,4,512]{3,1,2,0:T(1,128)S(1)}, u32[]{:S(2)}, u32[]{:S(2)}) collective-permute-start(f32[3,1,4,512]{3,1,2,0:T(1,128)S(1)} %slice.2934), channel_id=1, source_target_pairs={{0,124},{4,0},{8,4},{12,8},{16,12},{20,16},{24,20},{28,24},{32,28}... | collective-permute-start | bytes 73736 | tf_op jit(solution)/shard_map/ppermute | solution.py:18
  229.1 4.8 collective-permute-start.9
  273.9 2.7 collective-permute-start.10
  276.7 5.7 %collective-permute-start.11 = (f32[3,4,512]{2,0,1:T(4,128)S(1)}, f32[3,4,512]{2,0,1:T(4,128)S(1)}, u32[]{:S(2)}, u32[]{:S(2)}) collective-permute-start(f32[3,4,512]{2,0,1:T(4,128)S(1)} %bitcast.2175), channel_id=1, source_target_pairs={{0,4},{4,8},{8,12},{12,16},{16,20},{20,24},{24,28},{28,32},{32,36}... | collective-permute-start | bytes 73736 | tf_op jit(solution)/shard_map/ppermute | solution.py:18
  283.4 6.9 %collective-permute-start.12 = (f32[3,1,4,512]{3,1,2,0:T(1,128)S(1)}, f32[3,1,4,512]{3,1,2,0:T(1,128)S(1)}, u32[]{:S(2)}, u32[]{:S(2)}) collective-permute-start(f32[3,1,4,512]{3,1,2,0:T(1,128)S(1)} %slice.2981), channel_id=1, source_target_pairs={{0,124},{4,0},{8,4},{12,8},{16,12},{20,16},{24,20},{28,24},{32,28}... | collective-permute-start | bytes 73736 | tf_op jit(solution)/shard_map/ppermute | solution.py:18
  290.3 5.4 collective-permute-start.13
  338.4 22.3 %copy-start.11 = (f32[5,5,5,5,128]{4,1,3,2,0:T(8,128)S(1)}, f32[5,5,5,5,128]{4,1,3,2,0:T(8,128)}, u32[]{:S(2)}) copy-start(f32[5,5,5,5,128]{4,1,3,2,0:T(8,128)} %get-tuple-element.876) | copy-start | bytes 960004
  339.9 4.5 collective-permute-start.14
  344.5 3.5 collective-permute-start.15
  349.7 26.8 %copy-start.27 = (f32[3,4,4,512]{3,1,2,0:T(4,128)}, f32[3,4,4,512]{3,1,2,0:T(4,128)S(1)}, u32[]{:S(2)}) copy-start(f32[3,4,4,512]{3,1,2,0:T(4,128)S(1)} %get-tuple-element.601) | copy-start | bytes 294916
  352.5 6.9 %collective-permute-start.20 = (f32[3,1,4,512]{3,1,2,0:T(1,128)S(1)}, f32[3,1,4,512]{3,1,2,0:T(1,128)S(1)}, u32[]{:S(2)}, u32[]{:S(2)}) collective-permute-start(f32[3,1,4,512]{3,1,2,0:T(1,128)S(1)} %slice.3082), channel_id=1, source_target_pairs={{0,124},{4,0},{8,4},{12,8},{16,12},{20,16},{24,20},{28,24},{32,28}... | collective-permute-start | bytes 73736 | tf_op jit(solution)/shard_map/ppermute | solution.py:18
  359.4 5.4 collective-permute-start.21
  360.8 16.0 %copy-start.7 = (f32[3,5,5,5,5,1,1,128]{7,6,5,4,3,2,1,0:T(1,128)S(1)}, f32[3,5,5,5,5,1,1,128]{7,6,5,4,3,2,1,0:T(1,128)}, u32[]{:S(2)}) copy-start(f32[3,5,5,5,5,1,1,128]{7,6,5,4,3,2,1,0:T(1,128)} %param.85) | copy-start | bytes 2880004
  360.8 16.0 %copy-start.47 = (f32[3]{0:T(128)S(1)}, f32[3]{0:T(128)}, u32[]{:S(2)}) copy-start(f32[3]{0:T(128)} %copy-done.46) | copy-start | bytes 40
  402.3 15.4 %copy-start.17 = (f32[3,4,4,512]{3,1,2,0:T(4,128)S(1)}, f32[3,4,4,512]{3,1,2,0:T(4,128)}, u32[]{:S(2)}) copy-start(f32[3,4,4,512]{3,1,2,0:T(4,128)} %get-tuple-element.596) | copy-start | bytes 294916
  408.1 15.8 %copy-start.41 = (f32[4,512]{1,0:T(4,128)S(1)}, f32[4,512]{1,0:T(4,128)}, u32[]{:S(2)}) copy-start(f32[4,512]{1,0:T(4,128)} %get-tuple-element.576) | copy-start | bytes 24580
  409.6 4.4 collective-permute-start.22
  414.1 3.5 collective-permute-start.23
  417.9 6.9 %collective-permute-start.24 = (f32[3,1,4,512]{3,1,2,0:T(1,128)S(1)}, f32[3,1,4,512]{3,1,2,0:T(1,128)S(1)}, u32[]{:S(2)}, u32[]{:S(2)}) collective-permute-start(f32[3,1,4,512]{3,1,2,0:T(1,128)S(1)} %slice.3130), channel_id=1, source_target_pairs={{0,124},{4,0},{8,4},{12,8},{16,12},{20,16},{24,20},{28,24},{32,28}... | collective-permute-start | bytes 73736 | tf_op jit(solution)/shard_map/ppermute | solution.py:18
  424.8 5.4 collective-permute-start.25
  469.0 4.4 collective-permute-start.26
  473.5 3.5 collective-permute-start.27
  477.9 6.8 %collective-permute-start.28 = (f32[3,1,4,512]{3,1,2,0:T(1,128)S(1)}, f32[3,1,4,512]{3,1,2,0:T(1,128)S(1)}, u32[]{:S(2)}, u32[]{:S(2)}) collective-permute-start(f32[3,1,4,512]{3,1,2,0:T(1,128)S(1)} %slice.3179), channel_id=1, source_target_pairs={{0,124},{4,0},{8,4},{12,8},{16,12},{20,16},{24,20},{28,24},{32,28}... | collective-permute-start | bytes 73736 | tf_op jit(solution)/shard_map/ppermute | solution.py:18
  484.7 5.4 collective-permute-start.29
  527.0 15.4 %copy-start.34 = (f32[3,4,4,512]{3,1,2,0:T(4,128)S(1)}, f32[3,4,4,512]{3,1,2,0:T(4,128)}, u32[]{:S(2)}) copy-start(f32[3,4,4,512]{3,1,2,0:T(4,128)} %get-tuple-element.587) | copy-start | bytes 294916
  527.0 16.9 %copy-start.1 = (f32[256,64]{0,1:T(8,128)S(1)}, f32[256,64]{0,1:T(8,128)}, u32[]{:S(2)}) copy-start(f32[256,64]{0,1:T(8,128)} %param.93) | copy-start | bytes 196612
  534.3 4.4 collective-permute-start.30
  538.8 3.5 collective-permute-start.31
  (33 other events, 241.4 us)
where the time goes:
time: 555 us; the launch traced here: 544 us
  local copies, waits for them, and re-layouts  247 us (45%)
  other arithmetic  110 us (20%)
  starting transfers between devices  78.9 us (14%)
  waiting for transfers between devices  56.2 us (10%)
  matrix products  25.3 us (5%)
  blocking collectives  20.7 us (4%)
    slice x42, local copies, waits for them, and re-layouts, expand_axis(): lax.slice_in_dim(array, offset, offset + 4 * (elements - 1) + 1, stride=4...  72 us
    reshape x15, local copies, waits for them, and re-layouts, fold_axis(): jnp.stack([moved[0], moved[1], moved[2], moved[3]], axis=-1)  46.8 us
    reshape x8, local copies, waits for them, and re-layouts, fold_axis(): jnp.stack([moved[4], blank, blank, blank], axis=-1)  46.7 us
    ppermute x16, starting transfers between devices, shifted(): return lax.ppermute(value, axis, pairs)  44.9 us
    another operation x7, other arithmetic, fold_axis(): jnp.stack([moved[4], blank, blank, blank], axis=-1)  43.7 us
    ppermute x16, starting transfers between devices, shifted_2(): return lax.ppermute(block, axis, route)  34 us
    ppermute x16, waiting for transfers between devices, shifted_2(): return lax.ppermute(block, axis, route)  28.3 us
    ppermute x16, waiting for transfers between devices, shifted(): return lax.ppermute(value, axis, pairs)  28 us
  transfers between devices with their start and end apart: 32, of which 25 were waited for; matrix products, arithmetic and copies ran while one was open for 9% of the time, Pallas kernels for 0%

commit v1 on v0

v1 whole, which is shorter than its diff:
```python
import functools

import jax
import jax.numpy as jnp
import ml_dtypes
import numpy as np
from jax import lax
from jax.experimental import pallas as pl
from jax.experimental.pallas import tpu as pltpu
from jax.sharding import PartitionSpec as P

STEPS = 4
TAPS = 64
DT = 0.04
F32 = jnp.float32
BF16 = jnp.bfloat16
MESH = pl.DeviceIdType.MESH

DISP = (0, 3)
VEL = (6, 9)
RHO = 12
SLOTS = 13


def gll_tables():
    points = np.array([-1.0, -np.sqrt(3.0 / 7.0), 0.0, np.sqrt(3.0 / 7.0), 1.0])
    weights = np.array([0.1, 49.0 / 90.0, 32.0 / 45.0, 49.0 / 90.0, 0.1])
    products = np.array([np.prod([points[t] - points[o] for o in range(5) if o != t]) for t in range(5)])
    derivative = np.zeros((5, 5))
    for t in range(5):
        for s in range(5):
            if t == s:
                derivative[t, s] = np.sum([1.0 / (points[t] - points[o]) for o in range(5) if o != t])
            else:
                derivative[t, s] = products[t] / products[s] / (points[t] - points[s])
    return derivative, weights


DMAT, WGLL = gll_tables()


def node_row(b, c):
    return c * 5 + b if c < 4 else 24 + b


def halves(matrix):
    high = matrix.astype(ml_dtypes.bfloat16)
    low = (matrix - high.astype(np.float64)).astype(ml_dtypes.bfloat16)
    return high, low


def operators():
    same = np.zeros((32, 32))
    along_y = np.zeros((32, 32))
    along_z = np.zeros((32, 32))
    for b in range(5):
        for c in range(5):
            row = b * 5 + c
            same[row, node_row(b, c)] = 1.0
            for q in range(5):
                along_y[row, node_row(q, c)] = DMAT[b, q]
                along_z[row, node_row(b, q)] = DMAT[c, q]
    high, low = halves(np.concatenate([same, along_y, along_z], axis=0))
    gradient = np.concatenate([high, high, low], axis=1)
    y_high, y_low = halves(along_y.T)
    z_high, z_low = halves(along_z.T)
    back = same.T.astype(ml_dtypes.bfloat16)
    force = np.concatenate([y_high, z_high, y_high, z_high, y_low, z_low, back, back], axis=1)
    return gradient, force


def tables():
    table = np.zeros((5, 32, 128), np.float32)
    wn = np.array([0.2, 49.0 / 90.0, 32.0 / 45.0, 49.0 / 90.0, 0.2])
    for b in range(5):
        for c in range(5):
            table[0, b * 5 + c] = WGLL[b] * WGLL[c]
        for c in range(4):
            row = node_row(b, c)
            table[1, row] = 1.0 / (wn[b] * wn[c])
            table[2, row] = float(b == 0)
            table[3, row] = float(b == 4)
    table[4, 20:] = 1.0
    return table


def interleave():
    table = np.zeros((512, 512), np.float32)
    for c in range(4):
        for e in range(128):
            table[4 * e + c, c * 128 + e] = 1.0
    return table.astype(ml_dtypes.bfloat16)


def split2(x):
    high = x.astype(BF16)
    return high, (x - high.astype(F32)).astype(BF16)


def split3(x):
    high = x.astype(BF16)
    rest = x - high.astype(F32)
    middle = rest.astype(BF16)
    return high, middle, (rest - middle.astype(F32)).astype(BF16)


def derive(x, matrix):
    even = [x[0] + x[4], x[1] + x[3]]
    odd = [x[0] - x[4], x[1] - x[3]]
    out = [None] * 5
    for p in range(2):
        s = sum(float(0.5 * (matrix[p, q] - matrix[p, 4 - q])) * odd[q] for q in range(2))
        t = sum(float(0.5 * (matrix[p, q] + matrix[p, 4 - q])) * even[q] for q in range(2))
        t = t + float(matrix[p, 2]) * x[2]
        out[p] = s + t
        out[4 - p] = s - t
    out[2] = sum(float(matrix[2, q]) * odd[q] for q in range(2))
    return out


def kernel(
    ug, vg, rg, uc, vc, rc, lam, mu, defect, keep, rho, hist, cells, filt, perm, opg, opf, table,
    ug_o, vg_o, rg_o, uc_o, vc_o, rc_o,
    pair_u, pair_v, pair_r, perm_v, opg_v, opf_v, tab_v,
    mem, sw, qs, lam_v, mu_v, def_v, inv_mass,
    nd, ft, fs, yp, ym, rxm, rxp, rym, ryp, rdg,
    hy1, hy2, ry1, ry2, rc1, rc2,
    hist_v, cells_v, filt_v, fg_own, fgb, fgn, sj, frc,
    xr, out_v,
    lsem, osem, h_send, h_recv, f_send, f_recv, g_send, g_recv,
):
    s = lax.axis_index("slab")
    d = lax.axis_index("depth")
    ns = lax.axis_size("slab")
    nd_ = lax.axis_size("depth")
    sp, sm = lax.rem(s + 1, ns), lax.rem(s + ns - 1, ns)
    dp, dm = lax.rem(d + 1, nd_), lax.rem(d + nd_ - 1, nd_)

    barrier = pltpu.get_barrier_semaphore()
    peers = 0
    for ps in (s, sm, sp):
        for k in range(4):
            if ps is s and k == 0:
                continue
            pl.semaphore_signal(
                barrier, inc=1, device_id=(ps, lax.rem(d + k, nd_)), device_id_type=MESH
            )
            peers += 1

    loads = []

    def load(src, dst):
        copy = pltpu.make_async_copy(src, dst, lsem.at[len(loads)])
        copy.start()
        loads.append(copy)
        return copy

    l_ug = load(ug, pair_u.at[:, 0:4])
    l_uc = load(uc, pair_u.at[:, 4:8])
    l_perm = load(perm, perm_v)
    l_opg = load(opg, opg_v)
    l_tab = load(table, tab_v)
    l_vg = load(vg, pair_v.at[:, 0:4])
    l_vc = load(vc, pair_v.at[:, 4:8])
    l_rho = load(rho, pair_r.at[:, 0:4])
    l_opf = load(opf, opf_v)
    zero7 = jnp.zeros((7, 128), F32)
    for w in range(2):
        for k in range(75):
            mem[w, k, 25:32, :] = zero7
    for a in range(5):
        lam_v[a, 25:32, :] = zero7
        mu_v[a, 25:32, :] = zero7
        def_v[a, 25:32, :] = zero7
    for x in range(4):
        hist_v[x, 64:72, :] = jnp.zeros((8, 128), F32)
    l_lam = load(lam.at[:, :, 0], lam_v.at[:, 0:25])
    l_mu = load(mu.at[:, :, 0], mu_v.at[:, 0:25])
    l_rg = load(rg.at[:, :, 0], mem.at[0, :, 0:25])
    l_def = load(defect.at[:, :, 0], def_v.at[:, 0:25])
    l_cells = load(cells, cells_v)
    l_filt = load(filt, filt_v)
    l_hist = [load(hist.at[:, x], hist_v.at[x, 0:64]) for x in range(4)]
    l_rc = load(rc.at[:, :, 0], mem.at[1, :, 0:25])

    zero24 = jnp.zeros((24, 128), F32)
    for a in range(4):
        for k in range(SLOTS):
            nd[a, k] = zero24
    for q in range(8):
        fgn[pl.ds(q * 24, 24), :] = zero24

    def deinterleave(ref, blocks):
        rows = blocks * 8
        x = ref[...].reshape(rows, 512)
        y = jnp.dot(jnp.concatenate(split3(x), axis=0), perm_v[...], preferred_element_type=F32)
        return y[0:rows] + y[rows : 2 * rows] + y[2 * rows : 3 * rows]

    l_perm.wait()
    l_ug.wait()
    l_uc.wait()
    y = deinterleave(pair_u, 12)
    for k in range(12):
        for c in range(4):
            lanes = slice(c * 128, c * 128 + 128)
            nd[k % 4, DISP[0] + k // 4, c * 5 : c * 5 + 4, :] = y[k * 8 : k * 8 + 4, lanes]
            nd[k % 4, DISP[1] + k // 4, c * 5 : c * 5 + 4, :] = y[k * 8 + 4 : k * 8 + 8, lanes]
    for a in range(4):
        for k in range(3):
            hy1[a * 12 + k * 4 : a * 12 + k * 4 + 4, :] = nd[a, k, pl.ds(0, 4, stride=5), :]

    pl.semaphore_wait(barrier, peers)

    def remote(src, dst, send, recv, target):
        return pltpu.make_async_remote_copy(
            src_ref=src, dst_ref=dst, send_sem=send, recv_sem=recv, device_id=target, device_id_type=MESH
        )

    h1 = [
        remote(hy1, ry1, h_send.at[0], h_recv.at[0], (s, dm)),
        remote(nd.at[0, 0:3], nd.at[4, 0:3], h_send.at[1], h_recv.at[1], (sm, d)),
        remote(hy1.at[0:16], rc1, h_send.at[2], h_recv.at[2], (sm, dm)),
    ]
    for copy in h1:
        copy.start()

    l_vg.wait()
    l_vc.wait()
    l_rho.wait()
    y = deinterleave(pair_v, 12)
    for k in range(12):
        for c in range(4):
            lanes = slice(c * 128, c * 128 + 128)
            nd[k % 4, VEL[0] + k // 4, c * 5 : c * 5 + 4, :] = y[k * 8 : k * 8 + 4, lanes]
            nd[k % 4, VEL[1] + k // 4, c * 5 : c * 5 + 4, :] = y[k * 8 + 4 : k * 8 + 8, lanes]
    y = deinterleave(pair_r, 4)
    for k in range(4):
        for c in range(4):
            nd[k, RHO, c * 5 : c * 5 + 4, :] = y[k * 8 : k * 8 + 4, c * 128 : c * 128 + 128]
    for a in range(4):
        for k in range(10):
            row = a * 40 + k * 4
            hy2[row : row + 4, :] = nd[a, 3 + k, pl.ds(0, 4, stride=5), :]
    h2 = [
        remote(hy2, ry2, h_send.at[3], h_recv.at[3], (s, dm)),
        remote(nd.at[0, 3:13], nd.at[4, 3:13], h_send.at[4], h_recv.at[4], (sm, d)),
        remote(hy2.at[0:40], rc2, h_send.at[5], h_recv.at[5], (sm, dm)),
    ]
    for copy in h2:
        copy.start()

    l_tab.wait()
    l_lam.wait()
    l_mu.wait()
    l_def.wait()
    weight_bc = tab_v[0]
    for a in range(5):
        weight = weight_bc * float(WGLL[a])
        two_mu = 2.0 * mu_v[a]
        lam_v[a] = weight * lam_v[a]
        mu_v[a] = weight * two_mu
        def_v[a] = two_mu * def_v[a]

    def relaxed(w):
        for a in range(5):
            weight = weight_bc * float(WGLL[a])
            for k in range(5):
                j = k * 5 + a
                sw[w, j] = weight * (mem[w, j] + mem[w, 25 + j] + mem[w, 50 + j])

    l_rg.wait()
    relaxed(0)

    l_cells.wait()
    l_filt.wait()
    for copy in l_hist:
        copy.wait()
    filt3 = jnp.concatenate(split3(filt_v[...]), axis=0)
    ids = lax.broadcasted_iota(jnp.int32, (256, 128), 0)
    for x in range(4):
        one_hot = jnp.where(ids == cells_v[x : x + 1, :], 1.0, 0.0).astype(BF16)
        g = jnp.dot(filt3, one_hot, preferred_element_type=F32)
        g = g[0:64] + g[64:128] + g[128:192]
        for t in range(4):
            fg_own[x * 8 + t : x * 8 + t + 1, :] = jnp.sum(
                g * hist_v[x, t + 1 : t + 65, :], axis=0, keepdims=True
            )
            fg_own[x * 8 + 4 + t : x * 8 + 5 + t, :] = g[63 - t : 64 - t]
    far = remote(fg_own.at[0:8], fgb.at[d, 32:40], g_send.at[0], g_recv.at[4 + d], (sm, 0))
    far.start()

    @pl.when(d != 0)
    def _():
        remote(fg_own, fgb.at[d, 0:32], g_send.at[1], g_recv.at[d], (s, 0)).start()

    def strain_stress_force(w, t):
        opg_m = opg_v[...]
        comps = []
        for i in range(3):
            columns = []
            for a in range(5):
                u = nd[a, DISP[w] + i]
                u = jnp.concatenate([u, pltpu.roll(u[0:8], 127, 1)], axis=0)
                high, low = split2(u)
                columns.append(jnp.concatenate([high, low, high], axis=0))
            g = jnp.dot(opg_m, jnp.concatenate(columns, axis=1), preferred_element_type=F32)
            lanes = [slice(a * 128, a * 128 + 128) for a in range(5)]
            gx = derive([g[0:32, l] for l in lanes], DMAT)
            comps.append((gx, [g[32:64, l] for l in lanes], [g[64:96, l] for l in lanes]))
        fluxes = []
        for a in range(5):
            gx = [comps[i][0][a] for i in range(3)]
            gy = [comps[i][1][a] for i in range(3)]
            gz = [comps[i][2][a] for i in range(3)]
            xy = 0.5 * (gy[0] + gx[1])
            xz = 0.5 * (gz[0] + gx[2])
            yz = 0.5 * (gz[1] + gy[2])
            trace = gx[0] + gy[1] + gz[2]
            third = trace * (1.0 / 3.0)
            m, q = mu_v[a], def_v[a]
            for k, e in enumerate((gx[0] - third, gy[1] - third, xy, xz, yz)):
                qs[w, k * 5 + a] = q * e
            pressure = lam_v[a] * trace
            r = [sw[w, k * 5 + a] for k in range(5)]
            sxx = pressure + m * gx[0] - r[0]
            syy = pressure + m * gy[1] - r[1]
            szz = pressure + m * gz[2] + (r[0] + r[1])
            sxy = m * xy - r[2]
            sxz = m * xz - r[3]
            syz = m * yz - r[4]
            fluxes.append(((sxx, sxy, sxz), (sxy, syy, syz), (sxz, syz, szz)))
        opf_m = opf_v[...]
        for i in range(3):
            fx = derive([fluxes[a][0][i] for a in range(5)], DMAT.T)
            columns = []
            for a in range(5):
                y_high, y_low = split2(fluxes[a][1][i])
                z_high, z_low = split2(fluxes[a][2][i])
                x_high, x_low = split2(fx[a])
                columns.append(
                    jnp.concatenate([y_high, z_high, y_low, z_low, y_high, z_high, x_high, x_low], axis=0)
                )
            f = jnp.dot(opf_m, jnp.concatenate(columns, axis=1), preferred_element_type=F32)
            for a in range(5):
                fa = f[:, a * 128 : a * 128 + 128]
                fs[w, t, a, i, 0:8, :] = fa[0:8] + pltpu.roll(fa[24:32], 1, 1)
                fs[w, t, a, i, 8:24, :] = fa[8:24]

    below = (d < nd_ - 1).astype(F32)

    def messages(w, t):
        n = w * STEPS + t
        sends = [
            (ym.at[n], rym.at[n], (s, dm)),
            (yp.at[n], ryp.at[n], (s, dp)),
            (ym.at[n, 0:16], rdg.at[n, 0], (sm, dm)),
            (yp.at[n, 0:16], rdg.at[n, 1], (sm, dp)),
            (ym.at[n, 48:64], rdg.at[n, 2], (sp, dm)),
            (yp.at[n, 48:64], rdg.at[n, 3], (sp, dp)),
            (fs.at[w, t, 0], rxm.at[n], (sm, d)),
            (fs.at[w, t, 4], rxp.at[n], (sp, d)),
        ]
        return [
            remote(src, dst, f_send.at[n, j], f_recv.at[n, j], target)
            for j, (src, dst, target) in enumerate(sends)
        ]

    def send(w, t):
        n = w * STEPS + t
        for a in range(5):
            for i in range(3):
                row = a * 12 + i * 4
                ym[n, row : row + 4, :] = fs[w, t, a, i, pl.ds(0, 4, stride=5), :]
                yp[n, row : row + 4, :] = below * fs[w, t, a, i, pl.ds(4, 4, stride=5), :]
        ym[n, 60:64, :] = jnp.zeros((4, 128), F32)
        yp[n, 60:64, :] = jnp.zeros((4, 128), F32)
        for copy in messages(w, t):
            copy.start()

    kept = [keep[l] for l in range(3)]

    def memory(w, last):
        for a in range(5):
            weight = weight_bc * float(WGLL[a])
            for k in range(5):
                j = k * 5 + a
                q = qs[w, j]
                new = []
                for l in range(3):
                    value = kept[l] * mem[w, 25 * l + j] + (1.0 - kept[l]) * q
                    mem[w, 25 * l + j] = value
                    new.append(value)
                if not last:
                    sw[w, j] = weight * (new[0] + new[1] + new[2])

    def receive(w, t):
        n = w * STEPS + t
        for copy in messages(w, t):
            copy.wait_recv()
        for a in range(5):
            for i in range(3):
                f = fs[w, t, a, i]
                if a == 0:
                    f = f + rxp[n, i]
                if a == 4:
                    f = f + rxm[n, i]
                ft[a, i] = f
        for a in range(5):
            for i in range(3):
                row = a * 12 + i * 4
                low = ryp[n, row : row + 4, :]
                top = rym[n, row : row + 4, :]
                if a == 4:
                    low = low + rdg[n, 1, i * 4 : i * 4 + 4, :]
                    top = top + rdg[n, 0, i * 4 : i * 4 + 4, :]
                if a == 0:
                    low = low + rdg[n, 3, i * 4 : i * 4 + 4, :]
                    top = top + rdg[n, 2, i * 4 : i * 4 + 4, :]
                if w == 1 and i == 1:
                    low = low - frc[a * 4 : a * 4 + 4, :]
                at_low = (a, i, pl.ds(0, 4, stride=5), slice(None))
                at_top = (a, i, pl.ds(4, 4, stride=5), slice(None))
                ft[at_low] = ft[at_low] + low
                ft[at_top] = ft[at_top] + top

    def update(w):
        for a in range(5):
            scale = inv_mass[a]
            for i in range(3):
                v = nd[a, VEL[w] + i] - scale * ft[a, i]
                nd[a, VEL[w] + i] = v
                nd[a, DISP[w] + i] = nd[a, DISP[w] + i] + DT * v

    def sample(t):
        for a in range(5):
            sj[t, a * 4 : a * 4 + 4, :] = nd[a, DISP[0] + 1, pl.ds(0, 4, stride=5), :]

    def forcing(t):
        f = fgn[t * 24 : t * 24 + 24, :]
        for m in range(t + 1):
            f = f + fgn[(4 + m) * 24 : (5 + m) * 24, :] * sj[t - m]
        frc[...] = f

    for copy in h1:
        copy.wait()
    for a in range(4):
        for k in range(3):
            row = a * 12 + k * 4
            nd[a, k, pl.ds(4, 4, stride=5), :] = below * ry1[row : row + 4, :]
    for k in range(3):
        nd[4, k, pl.ds(4, 4, stride=5), :] = below * rc1[k * 4 : k * 4 + 4, :]
    l_opg.wait()
    l_opf.wait()
    strain_stress_force(0, 0)
    send(0, 0)

    l_rc.wait()
    relaxed(1)
    for copy in h2:
        copy.wait()
    for a in range(4):
        for k in range(10):
            row = a * 40 + k * 4
            top = ry2[row : row + 4, :]
            nd[a, 3 + k, pl.ds(4, 4, stride=5), :] = top if k == 9 else below * top
    for k in range(10):
        top = rc2[k * 4 : k * 4 + 4, :]
        nd[4, 3 + k, pl.ds(4, 4, stride=5), :] = top if k == 9 else below * top
    strain_stress_force(1, 0)
    send(1, 0)
    memory(0, False)
    first = (d == 0).astype(F32)
    row_factor = tab_v[1, 0:24] * (1.0 + first * tab_v[2, 0:24] - (1.0 - below) * tab_v[3, 0:24])
    for a in range(5):
        wx = float([0.2, 49.0 / 90.0, 32.0 / 45.0, 49.0 / 90.0, 0.2][a])
        inv_mass[a] = (DT / wx) * row_factor / (nd[a, RHO] + tab_v[4, 0:24])

    @pl.when(d == 0)
    def _():
        for j in range(1, 4):
            remote(fg_own, fgb.at[j, 0:32], g_send.at[1], g_recv.at[j], (s, 0)).wait_recv()
        for j in range(4):
            remote(fg_own.at[0:8], fgb.at[j, 32:40], g_send.at[0], g_recv.at[4 + j], (sm, 0)).wait_recv()
        fgb[0, 0:32, :] = fg_own[...]
        x = jnp.concatenate([fgb[j] for j in range(4)], axis=1)
        y = jnp.dot(jnp.concatenate(split3(x), axis=0), perm_v[...], preferred_element_type=F32)
        y = y[0:40] + y[40:80] + y[80:120]
        for a in range(5):
            for c in range(4):
                fgn[pl.ds(a * 4 + c, 8, stride=24), :] = y[a * 8 : a * 8 + 8, c * 128 : c * 128 + 128]

    far.wait_send()

    @pl.when(d != 0)
    def _():
        remote(fg_own, fgb.at[d, 0:32], g_send.at[1], g_recv.at[d], (s, 0)).wait_send()

    memory(1, False)

    stores = []

    def store(src, dst):
        copy = pltpu.make_async_copy(src, dst, osem.at[len(stores)])
        copy.start()
        stores.append(copy)

    def finish(w, u_out, v_out):
        for i in range(3):
            for x in range(4):
                row = (i * 4 + x) * 8
                for c in range(4):
                    xr[c, row : row + 4, :] = nd[x, DISP[w] + i, c * 5 : c * 5 + 4, :]
                    xr[c, row + 4 : row + 8, :] = nd[x, VEL[w] + i, c * 5 : c * 5 + 4, :]
        x = jnp.concatenate([xr[c] for c in range(4)], axis=1)
        y = lax.dot_general(
            jnp.concatenate(split3(x), axis=0), perm_v[...], (((1,), (1,)), ((), ())),
            preferred_element_type=F32,
        )
        out_v[w] = (y[0:96] + y[96:192] + y[192:288]).reshape(12, 8, 512)
        store(out_v.at[w, :, 0:4], u_out)
        store(out_v.at[w, :, 4:8], v_out)

    for t in range(STEPS):
        receive(0, t)
        update(0)
        sample(t)
        forcing(t)
        if t < STEPS - 1:
            strain_stress_force(0, t + 1)
            send(0, t + 1)
            if t > 0:
                memory(1, False)
        else:
            memory(1, True)
            store(mem.at[1, :, 0:25], rc_o.at[:, :, 0])
            finish(0, ug_o, vg_o)
        receive(1, t)
        update(1)
        if t < STEPS - 1:
            strain_stress_force(1, t + 1)
            send(1, t + 1)
            memory(0, t == STEPS - 2)
            if t == STEPS - 2:
                store(mem.at[0, :, 0:25], rg_o.at[:, :, 0])
        else:
            finish(1, uc_o, vc_o)
    for w in range(2):
        for t in range(STEPS):
            for copy in messages(w, t):
                copy.wait_send()
    for copy in stores:
        copy.wait()


def body(*args):
    (ug, vg, rg, uc, vc, rc, lam, mu, defect, keep, rho, hist, cells, filt) = args
    gradient, force = operators()
    operands = (
        ug.reshape(12, 4, 512), vg.reshape(12, 4, 512), rg.reshape(75, 25, 1, 128),
        uc.reshape(12, 4, 512), vc.reshape(12, 4, 512), rc.reshape(75, 25, 1, 128),
        lam.reshape(5, 25, 1, 128), mu.reshape(5, 25, 1, 128), defect.reshape(5, 25, 1, 128),
        keep, rho, hist, cells, filt.T,
        jnp.asarray(interleave()), jnp.asarray(gradient), jnp.asarray(force), jnp.asarray(tables()),
    )
    anywhere = pl.BlockSpec(memory_space=pl.ANY)
    in_specs = [anywhere] * len(operands)
    in_specs[9] = pl.BlockSpec(memory_space=pltpu.SMEM)
    nodal = jax.ShapeDtypeStruct((12, 4, 512), F32)
    points = jax.ShapeDtypeStruct((75, 25, 1, 128), F32)
    dma = pltpu.SemaphoreType.DMA
    vm = lambda *shape: pltpu.VMEM(shape, F32)
    waves = 2 * STEPS
    outs = pl.pallas_call(
        kernel,
        out_shape=(nodal, nodal, points, nodal, nodal, points),
        in_specs=in_specs,
        out_specs=(anywhere,) * 6,
        scratch_shapes=[
            vm(12, 8, 512), vm(12, 8, 512), vm(4, 8, 512),
            pltpu.VMEM((512, 512), BF16), pltpu.VMEM((96, 96), BF16), pltpu.VMEM((32, 256), BF16),
            vm(5, 32, 128),
            vm(2, 75, 32, 128), vm(2, 25, 32, 128), vm(2, 25, 32, 128),
            vm(5, 32, 128), vm(5, 32, 128), vm(5, 32, 128), vm(5, 24, 128),
            vm(5, SLOTS, 24, 128), vm(5, 3, 24, 128), vm(2, STEPS, 5, 3, 24, 128),
            vm(waves, 64, 128), vm(waves, 64, 128),
            vm(waves, 3, 24, 128), vm(waves, 3, 24, 128),
            vm(waves, 64, 128), vm(waves, 64, 128), vm(waves, 4, 16, 128),
            vm(48, 128), vm(160, 128), vm(48, 128), vm(160, 128), vm(16, 128), vm(40, 128),
            vm(4, 72, 128), pltpu.VMEM((4, 128), jnp.int32), vm(64, 256),
            vm(32, 128), vm(4, 40, 128), vm(192, 128), vm(STEPS, 24, 128), vm(24, 128),
            vm(4, 96, 128), vm(2, 12, 8, 512),
            dma((24,)), dma((6,)), dma((6,)), dma((6,)), dma((waves, 8)), dma((waves, 8)),
            dma((2,)), dma((8,)),
        ],
        compiler_params=pltpu.CompilerParams(
            collective_id=0, has_side_effects=True, vmem_limit_bytes=40 * 1024 * 1024
        ),
    )(*operands)
    full = (3, 5, 5, 5, 5, 1, 1, 128)
    u = (3, 4, 4, 512)
    return (
        outs[0].reshape(u), outs[1].reshape(u), outs[2].reshape(full),
        outs[3].reshape(u), outs[4].reshape(u), outs[5].reshape(full),
    )


def solution(mesh):
    nodal = P(None, "slab", "depth", None)
    points = P(None, None, None, None, None, "slab", "depth", None)
    material = P(None, None, None, "slab", "depth", None)
    return jax.shard_map(
        body,
        mesh=mesh,
        in_specs=(
            nodal, nodal, points, nodal, nodal, points, material, material, material, P(),
            P("slab", "depth", None), P(None, "slab", "depth"), P("slab", "depth"), P(),
        ),
        out_specs=(nodal, nodal, points, nodal, nodal, points),
        check_vma=False,
    )
```

time: 555 us -> 60.5 us (0.11); the launches traced: 544 us -> 59.7 us
  local copies, waits for them, and re-layouts: 247 us -> 18.8 us
  other arithmetic: 110 us -> 0 us
  starting transfers between devices: 78.9 us -> 0 us
  waiting for transfers between devices: 56.2 us -> 0 us
  Pallas kernels: 0 us -> 40.2 us
  matrix products: 25.3 us -> 0 us
  blocking collectives: 20.7 us -> 0 us
    reshape x24 -> x0, local copies, waits for them, and re-layouts: 93.8 us -> none  [the longest x15 46.8 us: fold_axis(): jnp.stack([moved[0], moved[1], moved[2], moved[3]], axis=-1)]
    slice x165 -> x0, local copies, waits for them, and re-layouts: 80.2 us -> none  [the longest x42 72 us: expand_axis(): lax.slice_in_dim(array, offset, offset + 4 * (elements - 1) + 1, stride=4...]
    ppermute x32 -> x0, starting transfers between devices: 78.9 us -> none  [the longest x16 44.9 us: shifted(): return lax.ppermute(value, axis, pairs)]
    another operation x75 -> x0, local copies, waits for them, and re-layouts: 60.2 us -> none  [the longest x25 27.3 us: fold_axis(): jnp.stack([moved[0], moved[1], moved[2], moved[3]], axis=-1)]
    ppermute x32 -> x0, waiting for transfers between devices: 56.2 us -> none  [the longest x16 28.3 us: shifted_2(): return lax.ppermute(block, axis, route)]
    another operation x51 -> x0, other arithmetic: 52.4 us -> none  [the longest x7 43.7 us: fold_axis(): jnp.stack([moved[4], blank, blank, blank], axis=-1)]
    pallas_call x0 -> x1, Pallas kernels: none -> 40.2 us  [body(): pl.pallas_call(kernel, out_shape=(nodal, nodal, points, nodal, nodal, poi...]
    dot_general x49 -> x0, matrix products: 25.3 us -> none  [the longest x8 5.66 us: element_force(): jnp.einsum('pq,ipbcxyz->iqbcxyz', derivative, flux_x, precision=highest)]
  transfers between devices with their start and end apart: 32 -> 0, of which waited for: 25 -> 0; matrix products, arithmetic and copies ran while one was open for 9% -> 0% of each run, Pallas kernels for 0% -> 0%
where the time goes in v1:
time: 60.5 us; the launch traced here: 59.7 us
  Pallas kernels  40.2 us (66%)
  local copies, waits for them, and re-layouts  18.8 us (31%)
  between operations  0.69 us (1%)
    pallas_call x1, Pallas kernels, body(): pl.pallas_call(kernel, out_shape=(nodal, nodal, points, nodal, nodal, poi...  40.2 us
    unnamed x42, local copies, waits for them, and re-layouts  18.8 us

profile of v1, /device:TPU:1, one launch (start us, length us, event | category | flops | bytes accessed | tf_op | source)
XLA Modules:
  0.0 59.7 jit_solution(10318024648624966839)
XLA Ops:
  0.6 0.0 copy-start.15
  0.7 0.0 copy-start.16
  0.7 0.0 copy-start.17
  0.7 0.7 %copy-done.15 = bf16[32,256]{1,0:T(8,128)(2,1)S(1)} copy-done((bf16[32,256]{1,0:T(8,128)(2,1)S(1)}, bf16[32,256]{1,0:T(8,128)(2,1)}, u32[]{:S(2)}) %copy-start.15) | copy-done | bytes 16408
  1.4 0.0 copy-done.16
  1.4 0.0 copy-done.17
  1.4 0.0 copy-start
  1.4 1.2 %copy-done = f32[3,5,5,5,5,1,1,128]{7,6,5,4,3,2,1,0:T(1,128)S(1)} copy-done((f32[3,5,5,5,5,1,1,128]{7,6,5,4,3,2,1,0:T(1,128)S(1)}, f32[3,5,5,5,5,1,1,128]{7,6,5,4,3,2,1,0:T(1,128)}, u32[]{:S(2)}) %copy-start) | copy-done | bytes 960024
  2.6 0.0 copy-start.1
  2.6 1.2 %copy-done.1 = f32[3,5,5,5,5,1,1,128]{7,6,5,4,3,2,1,0:T(1,128)S(1)} copy-done((f32[3,5,5,5,5,1,1,128]{7,6,5,4,3,2,1,0:T(1,128)S(1)}, f32[3,5,5,5,5,1,1,128]{7,6,5,4,3,2,1,0:T(1,128)}, u32[]{:S(2)}) %copy-start.1) | copy-done | bytes 960024
  3.8 0.0 copy-start.2
  3.8 1.0 %copy-done.2 = bf16[512,512]{1,0:T(8,128)(2,1)S(1)} copy-done((bf16[512,512]{1,0:T(8,128)(2,1)S(1)}, bf16[512,512]{1,0:T(8,128)(2,1)}, u32[]{:S(2)}) %copy-start.2) | copy-done | bytes 524312
  4.8 0.0 copy-start.3
  4.8 0.9 %copy-done.3 = f32[64,4,128]{2,1,0:T(4,128)S(1)} copy-done((f32[64,4,128]{2,1,0:T(4,128)S(1)}, f32[64,4,128]{2,1,0:T(4,128)}, u32[]{:S(2)}) %copy-start.3) | copy-done | bytes 131096
  5.7 0.0 copy-start.4
  5.7 0.9 %copy-done.4 = f32[3,4,4,512]{3,2,1,0:T(4,128)S(1)} copy-done((f32[3,4,4,512]{3,2,1,0:T(4,128)S(1)}, f32[3,4,4,512]{3,2,1,0:T(4,128)}, u32[]{:S(2)}) %copy-start.4) | copy-done | bytes 98328
  6.6 0.0 copy-start.5
  6.6 0.9 %copy-done.5 = f32[3,4,4,512]{3,2,1,0:T(4,128)S(1)} copy-done((f32[3,4,4,512]{3,2,1,0:T(4,128)S(1)}, f32[3,4,4,512]{3,2,1,0:T(4,128)}, u32[]{:S(2)}) %copy-start.5) | copy-done | bytes 98328
  7.5 0.0 copy-start.6
  7.5 0.9 %copy-done.6 = f32[3,4,4,512]{3,2,1,0:T(4,128)S(1)} copy-done((f32[3,4,4,512]{3,2,1,0:T(4,128)S(1)}, f32[3,4,4,512]{3,2,1,0:T(4,128)}, u32[]{:S(2)}) %copy-start.6) | copy-done | bytes 98328
  8.4 0.0 copy-start.7
  8.4 0.9 %copy-done.7 = f32[3,4,4,512]{3,2,1,0:T(4,128)S(1)} copy-done((f32[3,4,4,512]{3,2,1,0:T(4,128)S(1)}, f32[3,4,4,512]{3,2,1,0:T(4,128)}, u32[]{:S(2)}) %copy-start.7) | copy-done | bytes 98328
  9.3 0.0 copy-start.8
  9.3 0.9 %copy-done.8 = f32[5,32,128]{2,1,0:T(8,128)S(1)} copy-done((f32[5,32,128]{2,1,0:T(8,128)S(1)}, f32[5,32,128]{2,1,0:T(8,128)}, u32[]{:S(2)}) %copy-start.8) | copy-done | bytes 81944
  10.2 0.0 copy-start.9
  10.2 0.8 %copy-done.9 = f32[256,64]{0,1:T(8,128)S(1)} copy-done((f32[256,64]{0,1:T(8,128)S(1)}, f32[256,64]{0,1:T(8,128)}, u32[]{:S(2)}) %copy-start.9) | copy-done | bytes 65560
  11.0 0.0 copy-start.10
  11.0 0.8 %copy-done.10 = f32[5,5,5,1,1,128]{5,4,3,2,1,0:T(1,128)S(1)} copy-done((f32[5,5,5,1,1,128]{5,4,3,2,1,0:T(1,128)S(1)}, f32[5,5,5,1,1,128]{5,4,3,2,1,0:T(1,128)}, u32[]{:S(2)}) %copy-start.10) | copy-done | bytes 64024
  11.8 0.0 copy-start.11
  11.8 0.8 %copy-done.11 = f32[5,5,5,1,1,128]{5,4,3,2,1,0:T(1,128)S(1)} copy-done((f32[5,5,5,1,1,128]{5,4,3,2,1,0:T(1,128)S(1)}, f32[5,5,5,1,1,128]{5,4,3,2,1,0:T(1,128)}, u32[]{:S(2)}) %copy-start.11) | copy-done | bytes 64024
  12.7 0.0 copy-start.12
  12.7 0.8 %copy-done.12 = f32[5,5,5,1,1,128]{5,4,3,2,1,0:T(1,128)S(1)} copy-done((f32[5,5,5,1,1,128]{5,4,3,2,1,0:T(1,128)S(1)}, f32[5,5,5,1,1,128]{5,4,3,2,1,0:T(1,128)}, u32[]{:S(2)}) %copy-start.12) | copy-done | bytes 64024
  13.5 0.0 copy-start.13
  13.5 0.8 %copy-done.13 = f32[4,4,512]{2,1,0:T(4,128)S(1)} copy-done((f32[4,4,512]{2,1,0:T(4,128)S(1)}, f32[4,4,512]{2,1,0:T(4,128)}, u32[]{:S(2)}) %copy-start.13) | copy-done | bytes 32792
  14.3 0.0 copy-start.14
  14.3 0.7 %copy-done.14 = bf16[96,96]{1,0:T(8,128)(2,1)S(1)} copy-done((bf16[96,96]{1,0:T(8,128)(2,1)S(1)}, bf16[96,96]{1,0:T(8,128)(2,1)}, u32[]{:S(2)}) %copy-start.14) | copy-done | bytes 18456
  15.0 40.2 %shard_map.217 = (f32[12,4,512]{2,1,0:T(4,128)S(1)}, f32[12,4,512]{2,1,0:T(4,128)S(1)}, f32[75,25,1,128]{3,2,1,0:T(1,128)S(1)}, f32[12,4,512]{2,1,0:T(4,128)S(1)...) custom-call(f32[12,4,512]{2,1,0:T(4,128)S(1)} %bitcast.24, f32[12,4,512]{2,1,0:T(4,128)S(1)} %bitcast.25, ...), custom_call_target="tpu_custom_call" | custom-call | tf_op jit(solution)/shard_map/pallas_call | solution.py:573
  55.3 0.6 %copy.32 = f32[3,4,4,512]{3,2,1,0:T(4,128)} copy(f32[3,4,4,512]{3,2,1,0:T(4,128)S(1)} %bitcast.31) | data formatting | bytes 196608
  55.9 0.6 %copy.33 = f32[3,4,4,512]{3,2,1,0:T(4,128)} copy(f32[3,4,4,512]{3,2,1,0:T(4,128)S(1)} %bitcast.30) | data formatting | bytes 196608
  56.5 0.9 %copy.34 = f32[3,5,5,5,5,1,1,128]{7,6,5,4,3,2,1,0:T(1,128)} copy(f32[3,5,5,5,5,1,1,128]{7,6,5,4,3,2,1,0:T(1,128)S(1)} %bitcast.23) | data formatting | bytes 1920000
  57.5 0.6 %copy.35 = f32[3,4,4,512]{3,2,1,0:T(4,128)} copy(f32[3,4,4,512]{3,2,1,0:T(4,128)S(1)} %bitcast.29) | data formatting | bytes 196608
  58.1 0.6 %copy.36 = f32[3,4,4,512]{3,2,1,0:T(4,128)} copy(f32[3,4,4,512]{3,2,1,0:T(4,128)S(1)} %bitcast.28) | data formatting | bytes 196608
  58.8 0.9 %copy.37 = f32[3,5,5,5,5,1,1,128]{7,6,5,4,3,2,1,0:T(1,128)} copy(f32[3,5,5,5,5,1,1,128]{7,6,5,4,3,2,1,0:T(1,128)S(1)} %bitcast.22) | data formatting | bytes 1920000
Async XLA Ops:
  0.6 0.7 %copy-start.15 = (bf16[32,256]{1,0:T(8,128)(2,1)S(1)}, bf16[32,256]{1,0:T(8,128)(2,1)}, u32[]{:S(2)}) copy-start(bf16[32,256]{1,0:T(8,128)(2,1)} %constant.10.clone.opf) | copy-start | bytes 49156
  0.7 0.7 %copy-start.16 = (s32[4,128]{1,0:T(4,128)S(1)}, s32[4,128]{1,0:T(4,128)}, u32[]{:S(2)}) copy-start(s32[4,128]{1,0:T(4,128)} %cells.1) | copy-start | bytes 6148
  0.7 0.7 %copy-start.17 = (f32[3]{0:T(128)S(1)}, f32[3]{0:T(128)}, u32[]{:S(2)}) copy-start(f32[3]{0:T(128)} %keep.1) | copy-start | bytes 40
  1.4 1.2 %copy-start = (f32[3,5,5,5,5,1,1,128]{7,6,5,4,3,2,1,0:T(1,128)S(1)}, f32[3,5,5,5,5,1,1,128]{7,6,5,4,3,2,1,0:T(1,128)}, u32[]{:S(2)}) copy-start(f32[3,5,5,5,5,1,1,128]{7,6,5,4,3,2,1,0:T(1,128)} %param.20) | copy-start | bytes 2880004
  2.6 1.2 %copy-start.1 = (f32[3,5,5,5,5,1,1,128]{7,6,5,4,3,2,1,0:T(1,128)S(1)}, f32[3,5,5,5,5,1,1,128]{7,6,5,4,3,2,1,0:T(1,128)}, u32[]{:S(2)}) copy-start(f32[3,5,5,5,5,1,1,128]{7,6,5,4,3,2,1,0:T(1,128)} %param.23) | copy-start | bytes 2880004
  3.8 1.0 %copy-start.2 = (bf16[512,512]{1,0:T(8,128)(2,1)S(1)}, bf16[512,512]{1,0:T(8,128)(2,1)}, u32[]{:S(2)}) copy-start(bf16[512,512]{1,0:T(8,128)(2,1)} %constant.8.clone.perm) | copy-start | bytes 1572868
  4.8 0.9 %copy-start.3 = (f32[64,4,128]{2,1,0:T(4,128)S(1)}, f32[64,4,128]{2,1,0:T(4,128)}, u32[]{:S(2)}) copy-start(f32[64,4,128]{2,1,0:T(4,128)} %hist.1) | copy-start | bytes 393220
  5.7 0.9 %copy-start.4 = (f32[3,4,4,512]{3,2,1,0:T(4,128)S(1)}, f32[3,4,4,512]{3,2,1,0:T(4,128)}, u32[]{:S(2)}) copy-start(f32[3,4,4,512]{3,2,1,0:T(4,128)} %param.18) | copy-start | bytes 294916
  6.6 0.9 %copy-start.5 = (f32[3,4,4,512]{3,2,1,0:T(4,128)S(1)}, f32[3,4,4,512]{3,2,1,0:T(4,128)}, u32[]{:S(2)}) copy-start(f32[3,4,4,512]{3,2,1,0:T(4,128)} %param.19) | copy-start | bytes 294916
  7.5 0.9 %copy-start.6 = (f32[3,4,4,512]{3,2,1,0:T(4,128)S(1)}, f32[3,4,4,512]{3,2,1,0:T(4,128)}, u32[]{:S(2)}) copy-start(f32[3,4,4,512]{3,2,1,0:T(4,128)} %param.21) | copy-start | bytes 294916
  8.4 0.9 %copy-start.7 = (f32[3,4,4,512]{3,2,1,0:T(4,128)S(1)}, f32[3,4,4,512]{3,2,1,0:T(4,128)}, u32[]{:S(2)}) copy-start(f32[3,4,4,512]{3,2,1,0:T(4,128)} %param.22) | copy-start | bytes 294916
  9.3 0.9 %copy-start.8 = (f32[5,32,128]{2,1,0:T(8,128)S(1)}, f32[5,32,128]{2,1,0:T(8,128)}, u32[]{:S(2)}) copy-start(f32[5,32,128]{2,1,0:T(8,128)} %constant.11.clone.table) | copy-start | bytes 245764
  10.2 0.8 %copy-start.9 = (f32[256,64]{0,1:T(8,128)S(1)}, f32[256,64]{0,1:T(8,128)}, u32[]{:S(2)}) copy-start(f32[256,64]{0,1:T(8,128)} %param.31) | copy-start | bytes 196612
  11.0 0.8 %copy-start.10 = (f32[5,5,5,1,1,128]{5,4,3,2,1,0:T(1,128)S(1)}, f32[5,5,5,1,1,128]{5,4,3,2,1,0:T(1,128)}, u32[]{:S(2)}) copy-start(f32[5,5,5,1,1,128]{5,4,3,2,1,0:T(1,128)} %param.24) | copy-start | bytes 192004
  11.8 0.8 %copy-start.11 = (f32[5,5,5,1,1,128]{5,4,3,2,1,0:T(1,128)S(1)}, f32[5,5,5,1,1,128]{5,4,3,2,1,0:T(1,128)}, u32[]{:S(2)}) copy-start(f32[5,5,5,1,1,128]{5,4,3,2,1,0:T(1,128)} %param.25) | copy-start | bytes 192004
  12.7 0.8 %copy-start.12 = (f32[5,5,5,1,1,128]{5,4,3,2,1,0:T(1,128)S(1)}, f32[5,5,5,1,1,128]{5,4,3,2,1,0:T(1,128)}, u32[]{:S(2)}) copy-start(f32[5,5,5,1,1,128]{5,4,3,2,1,0:T(1,128)} %param.26) | copy-start | bytes 192004
  13.5 0.8 %copy-start.13 = (f32[4,4,512]{2,1,0:T(4,128)S(1)}, f32[4,4,512]{2,1,0:T(4,128)}, u32[]{:S(2)}) copy-start(f32[4,4,512]{2,1,0:T(4,128)} %rho.1) | copy-start | bytes 98308
  14.3 0.7 %copy-start.14 = (bf16[96,96]{1,0:T(8,128)(2,1)S(1)}, bf16[96,96]{1,0:T(8,128)(2,1)}, u32[]{:S(2)}) copy-start(bf16[96,96]{1,0:T(8,128)(2,1)} %constant.9.clone.opg) | copy-start | bytes 55300

commit v2 on v1

--- a/solution.py
+++ b/solution.py
@@ -120,14 +120,14 @@
 
 def kernel(
     ug, vg, rg, uc, vc, rc, lam, mu, defect, keep, rho, hist, cells, filt, perm, opg, opf, table,
-    ug_o, vg_o, rg_o, uc_o, vc_o, rc_o,
+    mem, out_v,
     pair_u, pair_v, pair_r, perm_v, opg_v, opf_v, tab_v,
-    mem, sw, qs, lam_v, mu_v, def_v, inv_mass,
+    sw, qs, lam_v, mu_v, def_v, inv_mass,
     nd, ft, fs, yp, ym, rxm, rxp, rym, ryp, rdg,
     hy1, hy2, ry1, ry2, rc1, rc2,
     hist_v, cells_v, filt_v, fg_own, fgb, fgn, sj, frc,
-    xr, out_v,
-    lsem, osem, h_send, h_recv, f_send, f_recv, g_send, g_recv,
+    xr,
+    keep_s, lsem, h_send, h_recv, f_send, f_recv, g_send, g_recv,
 ):
     s = lax.axis_index("slab")
     d = lax.axis_index("depth")
@@ -178,6 +178,7 @@
     l_mu = load(mu.at[:, :, 0], mu_v.at[:, 0:25])
     l_rg = load(rg.at[:, :, 0], mem.at[0, :, 0:25])
     l_def = load(defect.at[:, :, 0], def_v.at[:, 0:25])
+    l_keep = load(keep, keep_s)
     l_cells = load(cells, cells_v)
     l_filt = load(filt, filt_v)
     l_hist = [load(hist.at[:, x], hist_v.at[x, 0:64]) for x in range(4)]
@@ -377,7 +378,8 @@
         for copy in messages(w, t):
             copy.start()
 
-    kept = [keep[l] for l in range(3)]
+    l_keep.wait()
+    kept = [keep_s[l] for l in range(3)]
 
     def memory(w, last):
         for a in range(5):
@@ -497,14 +499,7 @@
 
     memory(1, False)
 
-    stores = []
-
-    def store(src, dst):
-        copy = pltpu.make_async_copy(src, dst, osem.at[len(stores)])
-        copy.start()
-        stores.append(copy)
-
-    def finish(w, u_out, v_out):
+    def finish(w):
         for i in range(3):
             for x in range(4):
                 row = (i * 4 + x) * 8
@@ -517,8 +512,6 @@
             preferred_element_type=F32,
         )
         out_v[w] = (y[0:96] + y[96:192] + y[192:288]).reshape(12, 8, 512)
-        store(out_v.at[w, :, 0:4], u_out)
-        store(out_v.at[w, :, 4:8], v_out)
 
     for t in range(STEPS):
         receive(0, t)
@@ -532,23 +525,34 @@
                 memory(1, False)
         else:
             memory(1, True)
-            store(mem.at[1, :, 0:25], rc_o.at[:, :, 0])
-            finish(0, ug_o, vg_o)
+            finish(0)
         receive(1, t)
         update(1)
         if t < STEPS - 1:
             strain_stress_force(1, t + 1)
             send(1, t + 1)
             memory(0, t == STEPS - 2)
-            if t == STEPS - 2:
-                store(mem.at[0, :, 0:25], rg_o.at[:, :, 0])
         else:
-            finish(1, uc_o, vc_o)
+            finish(1)
     for w in range(2):
         for t in range(STEPS):
             for copy in messages(w, t):
                 copy.wait_send()
-    for copy in stores:
+
+
+def write_kernel(mem, out_v, ug_o, vg_o, rg_o, uc_o, vc_o, rc_o, sem):
+    pairs = [
+        (mem.at[0, :, 0:25], rg_o.at[:, :, 0]),
+        (mem.at[1, :, 0:25], rc_o.at[:, :, 0]),
+        (out_v.at[0, :, 0:4], ug_o),
+        (out_v.at[0, :, 4:8], vg_o),
+        (out_v.at[1, :, 0:4], uc_o),
+        (out_v.at[1, :, 4:8], vc_o),
+    ]
+    copies = [pltpu.make_async_copy(src, dst, sem.at[j]) for j, (src, dst) in enumerate(pairs)]
+    for copy in copies:
+        copy.start()
+    for copy in copies:
         copy.wait()
 
 
@@ -562,24 +566,27 @@
         keep, rho, hist, cells, filt.T,
         jnp.asarray(interleave()), jnp.asarray(gradient), jnp.asarray(force), jnp.asarray(tables()),
     )
-    anywhere = pl.BlockSpec(memory_space=pl.ANY)
-    in_specs = [anywhere] * len(operands)
-    in_specs[9] = pl.BlockSpec(memory_space=pltpu.SMEM)
-    nodal = jax.ShapeDtypeStruct((12, 4, 512), F32)
-    points = jax.ShapeDtypeStruct((75, 25, 1, 128), F32)
+    operands = tuple(
+        pltpu.with_memory_space_constraint(x, pltpu.HBM) for x in operands
+    )
+    in_hbm = pl.BlockSpec(memory_space=pltpu.HBM)
+    in_vmem = pl.BlockSpec(memory_space=pltpu.VMEM)
+    in_specs = [in_hbm] * len(operands)
+    nodal = pltpu.HBM((12, 4, 512), F32)
+    points = pltpu.HBM((75, 25, 1, 128), F32)
     dma = pltpu.SemaphoreType.DMA
     vm = lambda *shape: pltpu.VMEM(shape, F32)
     waves = 2 * STEPS
-    outs = pl.pallas_call(
+    results = pl.pallas_call(
         kernel,
-        out_shape=(nodal, nodal, points, nodal, nodal, points),
+        out_shape=(vm(2, 75, 32, 128), vm(2, 12, 8, 512)),
         in_specs=in_specs,
-        out_specs=(anywhere,) * 6,
+        out_specs=(in_vmem,) * 2,
         scratch_shapes=[
             vm(12, 8, 512), vm(12, 8, 512), vm(4, 8, 512),
             pltpu.VMEM((512, 512), BF16), pltpu.VMEM((96, 96), BF16), pltpu.VMEM((32, 256), BF16),
             vm(5, 32, 128),
-            vm(2, 75, 32, 128), vm(2, 25, 32, 128), vm(2, 25, 32, 128),
+            vm(2, 25, 32, 128), vm(2, 25, 32, 128),
             vm(5, 32, 128), vm(5, 32, 128), vm(5, 32, 128), vm(5, 24, 128),
             vm(5, SLOTS, 24, 128), vm(5, 3, 24, 128), vm(2, STEPS, 5, 3, 24, 128),
             vm(waves, 64, 128), vm(waves, 64, 128),
@@ -588,14 +595,22 @@
             vm(48, 128), vm(160, 128), vm(48, 128), vm(160, 128), vm(16, 128), vm(40, 128),
             vm(4, 72, 128), pltpu.VMEM((4, 128), jnp.int32), vm(64, 256),
             vm(32, 128), vm(4, 40, 128), vm(192, 128), vm(STEPS, 24, 128), vm(24, 128),
-            vm(4, 96, 128), vm(2, 12, 8, 512),
-            dma((24,)), dma((6,)), dma((6,)), dma((6,)), dma((waves, 8)), dma((waves, 8)),
+            vm(4, 96, 128),
+            pltpu.SMEM((3,), F32), dma((24,)), dma((6,)), dma((6,)), dma((waves, 8)), dma((waves, 8)),
             dma((2,)), dma((8,)),
         ],
         compiler_params=pltpu.CompilerParams(
             collective_id=0, has_side_effects=True, vmem_limit_bytes=40 * 1024 * 1024
         ),
     )(*operands)
+    outs = pl.pallas_call(
+        write_kernel,
+        out_shape=(nodal, nodal, points, nodal, nodal, points),
+        in_specs=(in_vmem,) * 2,
+        out_specs=(in_hbm,) * 6,
+        scratch_shapes=[dma((6,))],
+        compiler_params=pltpu.CompilerParams(vmem_limit_bytes=1024 * 1024),
+    )(*(pltpu.with_memory_space_constraint(x, pltpu.VMEM) for x in results))
     full = (3, 5, 5, 5, 5, 1, 1, 128)
     u = (3, 4, 4, 512)
     return (

time: 60.5 us -> 41.9 us (0.69); the launches traced: 59.7 us -> 41.8 us
  local copies, waits for them, and re-layouts: 18.8 us -> 0 us
  Pallas kernels: 40.2 us -> 41.1 us
    unnamed x42 -> x0, local copies, waits for them, and re-layouts: 18.8 us -> none
    pallas_call x1 -> x2, Pallas kernels: 40.2 us -> 41.1 us  [the longest x1 39.7 us: body(): pl.pallas_call(kernel, out_shape=(vm(2, 75, 32, 128), vm(2, 12, 8, 512)),...]
where the time goes in v2:
time: 41.9 us; the launch traced here: 41.8 us
  Pallas kernels  41.1 us (98%)
  between operations  0.65 us (2%)
    pallas_call x1, Pallas kernels, body(): pl.pallas_call(kernel, out_shape=(vm(2, 75, 32, 128), vm(2, 12, 8, 512)),...  39.7 us
    pallas_call x1, Pallas kernels, body(): pl.pallas_call(write_kernel, out_shape=(nodal, nodal, points, nodal, noda...  1.42 us

profile of v2, /device:TPU:1, one launch (start us, length us, event | category | flops | bytes accessed | tf_op | source)
XLA Modules:
  0.0 41.8 jit_solution(17443865201381166720)
XLA Ops:
  0.6 39.7 %shard_map.217 = (f32[2,75,32,128]{3,2,1,0:T(8,128)S(1)}, f32[2,12,8,512]{3,2,1,0:T(8,128)S(1)}) custom-call(f32[12,4,512]{2,1,0:T(4,128)} %bitcast.22, f32[12,4,512]{2,1,0:T(4,128)} %bitcast.23, f32[75,25,1,128]{3,2,1,0:T(1,128)} %bitcast.20, f32[12,4,512]{2,1,0:T(4,128)} %bitcast.24, f32[12,4,512]{2,1,0:T(4,128)} %bitcast.25, f32[75,25,1,128]{3,2,1,0:T(1,128)} %bitcast.21, ...), custom_call_target="tpu_custom_call" | custom-call | tf_op jit(solution)/shard_map/pallas_call | solution.py:580
  40.3 1.4 %shard_map.218 = (f32[12,4,512]{2,1,0:T(4,128)}, f32[12,4,512]{2,1,0:T(4,128)}, f32[75,25,1,128]{3,2,1,0:T(1,128)}, f32[12,4,512]{2,1,0:T(4,128)}, f32[12,4,512]{2,1,0:T(4,128)}, /*index=5*/f32[75,25,1,128]{3,2,1,0:T(1,128)}) custom-call(f32[2,75,32,128]{3,2,1,0:T(8,128)S(1)} %get-tuple-element.14.mem, f32[2,12,8,512]{3,2,1,0:T(8,128)S(1)} %get-tuple-element.15.out_v), custom_call_target="tpu_custom_call" | custom-call | tf_op jit(solution)/shard_map/pallas_call | solution.py:606

commit v3 on v2

--- a/solution.py
+++ b/solution.py
@@ -134,18 +134,34 @@
     ns = lax.axis_size("slab")
     nd_ = lax.axis_size("depth")
     sp, sm = lax.rem(s + 1, ns), lax.rem(s + ns - 1, ns)
-    dp, dm = lax.rem(d + 1, nd_), lax.rem(d + nd_ - 1, nd_)
+    dp, dm = d + 1, d - 1
 
     barrier = pltpu.get_barrier_semaphore()
-    peers = 0
-    for ps in (s, sm, sp):
-        for k in range(4):
-            if ps is s and k == 0:
-                continue
-            pl.semaphore_signal(
-                barrier, inc=1, device_id=(ps, lax.rem(d + k, nd_)), device_id_type=MESH
-            )
-            peers += 1
+
+    def greet(*target):
+        pl.semaphore_signal(barrier, inc=1, device_id=target, device_id_type=MESH)
+
+    has_low, has_top = d > 0, d < nd_ - 1
+
+    @pl.when(d == 0)
+    def _():
+        for k in (3, 2):
+            greet(sp, k)
+            greet(s, k)
+
+    @pl.when(has_low)
+    def _():
+        for x in (sm, sp, s):
+            greet(x, dm)
+
+    @pl.when(has_top)
+    def _():
+        for x in (sm, sp, s):
+            greet(x, dp)
+
+    greet(sm, d)
+    greet(sp, d)
+    peers = 2 + 3 * has_low.astype(jnp.int32) + 3 * has_top.astype(jnp.int32) + 2 * (d >= 2).astype(jnp.int32)
 
     loads = []
 
@@ -217,13 +233,43 @@
             src_ref=src, dst_ref=dst, send_sem=send, recv_sem=recv, device_id=target, device_id_type=MESH
         )
 
-    h1 = [
-        remote(hy1, ry1, h_send.at[0], h_recv.at[0], (s, dm)),
-        remote(nd.at[0, 0:3], nd.at[4, 0:3], h_send.at[1], h_recv.at[1], (sm, d)),
-        remote(hy1.at[0:16], rc1, h_send.at[2], h_recv.at[2], (sm, dm)),
-    ]
-    for copy in h1:
-        copy.start()
+    def halo(first, slots, rows, recv_rows, corner):
+        h = 0 if first else 3
+        size = corner.shape[0]
+        low = [
+            remote(rows.at[0:size], corner, h_send.at[h + 2], h_recv.at[h + 2], (sm, dm)),
+            remote(rows, recv_rows, h_send.at[h], h_recv.at[h], (s, dm)),
+        ]
+        side = remote(nd.at[0, slots], nd.at[4, slots], h_send.at[h + 1], h_recv.at[h + 1], (sm, d))
+        return low, side
+
+    def halo_start(*args):
+        low, side = halo(*args)
+
+        @pl.when(has_low)
+        def _():
+            for copy in low:
+                copy.start()
+
+        side.start()
+
+    def halo_wait(*args):
+        low, side = halo(*args)
+        side.wait()
+
+        @pl.when(has_low)
+        def _():
+            for copy in low:
+                copy.wait_send()
+
+        @pl.when(has_top)
+        def _():
+            for copy in low:
+                copy.wait_recv()
+
+    h1 = (True, slice(0, 3), hy1, ry1, rc1)
+    h2 = (False, slice(3, 13), hy2, ry2, rc2)
+    halo_start(*h1)
 
     l_vg.wait()
     l_vc.wait()
@@ -242,13 +288,23 @@
         for k in range(10):
             row = a * 40 + k * 4
             hy2[row : row + 4, :] = nd[a, 3 + k, pl.ds(0, 4, stride=5), :]
-    h2 = [
-        remote(hy2, ry2, h_send.at[3], h_recv.at[3], (s, dm)),
-        remote(nd.at[0, 3:13], nd.at[4, 3:13], h_send.at[4], h_recv.at[4], (sm, d)),
-        remote(hy2.at[0:40], rc2, h_send.at[5], h_recv.at[5], (sm, dm)),
-    ]
-    for copy in h2:
-        copy.start()
+    halo_start(*h2)
+
+    @pl.when(d == nd_ - 1)
+    def _():
+        for ref in (ry1, ry2, rc1, rc2):
+            ref[...] = jnp.ones(ref.shape, F32)
+        for n in range(2 * STEPS):
+            rym[n] = jnp.zeros((64, 128), F32)
+            rdg[n, 0] = jnp.zeros((16, 128), F32)
+            rdg[n, 2] = jnp.zeros((16, 128), F32)
+
+    @pl.when(d == 0)
+    def _():
+        for n in range(2 * STEPS):
+            ryp[n] = jnp.zeros((64, 128), F32)
+            rdg[n, 1] = jnp.zeros((16, 128), F32)
+            rdg[n, 3] = jnp.zeros((16, 128), F32)
 
     l_tab.wait()
     l_lam.wait()
@@ -351,20 +407,61 @@
 
     def messages(w, t):
         n = w * STEPS + t
-        sends = [
+        low = [
+            (ym.at[n, 0:16], rdg.at[n, 0], (sm, dm)),
+            (ym.at[n, 48:64], rdg.at[n, 2], (sp, dm)),
             (ym.at[n], rym.at[n], (s, dm)),
+        ]
+        top = [
+            (yp.at[n, 0:16], rdg.at[n, 1], (sm, dp)),
+            (yp.at[n, 48:64], rdg.at[n, 3], (sp, dp)),
             (yp.at[n], ryp.at[n], (s, dp)),
-            (ym.at[n, 0:16], rdg.at[n, 0], (sm, dm)),
-            (yp.at[n, 0:16], rdg.at[n, 1], (sm, dp)),
-            (ym.at[n, 48:64], rdg.at[n, 2], (sp, dm)),
-            (yp.at[n, 48:64], rdg.at[n, 3], (sp, dp)),
+        ]
+        side = [
             (fs.at[w, t, 0], rxm.at[n], (sm, d)),
             (fs.at[w, t, 4], rxp.at[n], (sp, d)),
         ]
-        return [
-            remote(src, dst, f_send.at[n, j], f_recv.at[n, j], target)
-            for j, (src, dst, target) in enumerate(sends)
-        ]
+        made = []
+        for base, group in ((0, low), (3, top), (6, side)):
+            made.append(
+                [
+                    remote(src, dst, f_send.at[n, base + j], f_recv.at[n, base + j], target)
+                    for j, (src, dst, target) in enumerate(group)
+                ]
+            )
+        return made
+
+    def start_all(w, t):
+        low, top, side = messages(w, t)
+
+        @pl.when(has_low)
+        def _():
+            for copy in low:
+                copy.start()
+
+        @pl.when(has_top)
+        def _():
+            for copy in top:
+                copy.start()
+
+        for copy in side:
+            copy.start()
+
+    def wait_all(w, t, name):
+        low, top, side = messages(w, t)
+        for copy in side:
+            getattr(copy, name)()
+        sent = name == "wait_send"
+
+        @pl.when(has_low if sent else has_top)
+        def _():
+            for copy in low:
+                getattr(copy, name)()
+
+        @pl.when(has_top if sent else has_low)
+        def _():
+            for copy in top:
+                getattr(copy, name)()
 
     def send(w, t):
         n = w * STEPS + t
@@ -372,11 +469,10 @@
             for i in range(3):
                 row = a * 12 + i * 4
                 ym[n, row : row + 4, :] = fs[w, t, a, i, pl.ds(0, 4, stride=5), :]
-                yp[n, row : row + 4, :] = below * fs[w, t, a, i, pl.ds(4, 4, stride=5), :]
+                yp[n, row : row + 4, :] = fs[w, t, a, i, pl.ds(4, 4, stride=5), :]
         ym[n, 60:64, :] = jnp.zeros((4, 128), F32)
         yp[n, 60:64, :] = jnp.zeros((4, 128), F32)
-        for copy in messages(w, t):
-            copy.start()
+        start_all(w, t)
 
     l_keep.wait()
     kept = [keep_s[l] for l in range(3)]
@@ -397,8 +493,7 @@
 
     def receive(w, t):
         n = w * STEPS + t
-        for copy in messages(w, t):
-            copy.wait_recv()
+        wait_all(w, t, "wait_recv")
         for a in range(5):
             for i in range(3):
                 f = fs[w, t, a, i]
@@ -443,8 +538,7 @@
             f = f + fgn[(4 + m) * 24 : (5 + m) * 24, :] * sj[t - m]
         frc[...] = f
 
-    for copy in h1:
-        copy.wait()
+    halo_wait(*h1)
     for a in range(4):
         for k in range(3):
             row = a * 12 + k * 4
@@ -458,8 +552,7 @@
 
     l_rc.wait()
     relaxed(1)
-    for copy in h2:
-        copy.wait()
+    halo_wait(*h2)
     for a in range(4):
         for k in range(10):
             row = a * 40 + k * 4
@@ -536,8 +629,7 @@
             finish(1)
     for w in range(2):
         for t in range(STEPS):
-            for copy in messages(w, t):
-                copy.wait_send()
+            wait_all(w, t, "wait_send")
 
 
 def write_kernel(mem, out_v, ug_o, vg_o, rg_o, uc_o, vc_o, rc_o, sem):

time: 41.9 us -> 38.2 us (0.912)
  Pallas kernels: 41.1 us -> 37.5 us
    pallas_call x1, Pallas kernels: 39.7 us -> 36.1 us  [body(): pl.pallas_call(kernel, out_shape=(vm(2, 75, 32, 128), vm(2, 12, 8, 512)),...]
where the time goes in v3:
time: 38.2 us; the launch traced here: 38.1 us
  Pallas kernels  37.5 us (98%)
  between operations  0.65 us (2%)
    pallas_call x1, Pallas kernels, body(): pl.pallas_call(kernel, out_shape=(vm(2, 75, 32, 128), vm(2, 12, 8, 512)),...  36.1 us
    pallas_call x1, Pallas kernels, body(): pl.pallas_call(write_kernel, out_shape=(nodal, nodal, points, nodal, noda...  1.42 us

profile of v3, /device:TPU:1, one launch (start us, length us, event | category | flops | bytes accessed | tf_op | source)
XLA Modules:
  0.0 38.1 jit_solution(2677801036885566396)
XLA Ops:
  0.6 36.1 %shard_map.217 = (f32[2,75,32,128]{3,2,1,0:T(8,128)S(1)}, f32[2,12,8,512]{3,2,1,0:T(8,128)S(1)}) custom-call(f32[12,4,512]{2,1,0:T(4,128)} %bitcast.22, f32[12,4,512]{2,1,0:T(4,128)} %bitcast.23, f32[75,25,1,128]{3,2,1,0:T(1,128)} %bitcast.20, f32[12,4,512]{2,1,0:T(4,128)} %bitcast.24, f32[12,4,512]{2,1,0:T(4,128)} %bitcast.25, f32[75,25,1,128]{3,2,1,0:T(1,128)} %bitcast.21, ...), custom_call_target="tpu_custom_call" | custom-call | tf_op jit(solution)/shard_map/pallas_call | solution.py:672
  36.7 1.4 %shard_map.218 = (f32[12,4,512]{2,1,0:T(4,128)}, f32[12,4,512]{2,1,0:T(4,128)}, f32[75,25,1,128]{3,2,1,0:T(1,128)}, f32[12,4,512]{2,1,0:T(4,128)}, f32[12,4,512]{2,1,0:T(4,128)}, /*index=5*/f32[75,25,1,128]{3,2,1,0:T(1,128)}) custom-call(f32[2,75,32,128]{3,2,1,0:T(8,128)S(1)} %get-tuple-element.14.mem, f32[2,12,8,512]{3,2,1,0:T(8,128)S(1)} %get-tuple-element.15.out_v), custom_call_target="tpu_custom_call" | custom-call | tf_op jit(solution)/shard_map/pallas_call | solution.py:698

commit v4 on v3

--- a/solution.py
+++ b/solution.py
@@ -15,6 +15,7 @@
 F32 = jnp.float32
 BF16 = jnp.bfloat16
 MESH = pl.DeviceIdType.MESH
+ROW = 8
 
 DISP = (0, 3)
 VEL = (6, 9)
@@ -124,10 +125,10 @@
     pair_u, pair_v, pair_r, perm_v, opg_v, opf_v, tab_v,
     sw, qs, lam_v, mu_v, def_v, inv_mass,
     nd, ft, fs, yp, ym, rxm, rxp, rym, ryp, rdg,
-    hy1, hy2, ry1, ry2, rc1, rc2,
+    hy0, hy1, hy2, ry0, ry1, ry2, rc0, rc1, rc2, rlp, rl0, rl1, rl2,
     hist_v, cells_v, filt_v, fg_own, fgb, fgn, sj, frc,
     xr,
-    keep_s, lsem, h_send, h_recv, f_send, f_recv, g_send, g_recv,
+    keep_s, lsem, ready, h_send, h_recv, l_send, l_recv, f_send, f_recv, g_send, g_recv,
 ):
     s = lax.axis_index("slab")
     d = lax.axis_index("depth")
@@ -143,25 +144,65 @@
 
     has_low, has_top = d > 0, d < nd_ - 1
 
+    head, relay, tail = (lax.rem(s, ROW) == k for k in (0, 1, ROW - 1))
+    not_head, not_tail = jnp.logical_not(head), jnp.logical_not(tail)
+    row_before, row_after = lax.rem(s + ns - ROW + 1, ns), lax.rem(s + ROW - 1, ns)
+
+    @pl.when(relay)
+    def _():
+        greet(row_after, d)
+
+        @pl.when(has_top)
+        def _():
+            greet(row_after, dp)
+
+    @pl.when(tail)
+    def _():
+        greet(s - (ROW - 2), d)
+
+    @pl.when(jnp.logical_and(head, d >= 2))
+    def _():
+        greet(sm, 0)
+
+    @pl.when(not_tail)
+    def _():
+        @pl.when(d == 0)
+        def _():
+            for k in (3, 2):
+                greet(sp, k)
+
+        @pl.when(has_low)
+        def _():
+            greet(sp, dm)
+
+        @pl.when(has_top)
+        def _():
+            greet(sp, dp)
+
+        greet(sp, d)
+
     @pl.when(d == 0)
     def _():
         for k in (3, 2):
-            greet(sp, k)
             greet(s, k)
 
     @pl.when(has_low)
     def _():
-        for x in (sm, sp, s):
-            greet(x, dm)
+        greet(sm, dm)
+        greet(s, dm)
 
     @pl.when(has_top)
     def _():
-        for x in (sm, sp, s):
-            greet(x, dp)
+        greet(sm, dp)
+        greet(s, dp)
 
     greet(sm, d)
-    greet(sp, d)
-    peers = 2 + 3 * has_low.astype(jnp.int32) + 3 * has_top.astype(jnp.int32) + 2 * (d >= 2).astype(jnp.int32)
+    low_n, top_n, far_n = (flag.astype(jnp.int32) for flag in (has_low, has_top, d >= 2))
+    usual = 2 + 3 * low_n + 3 * top_n + 2 * far_n
+    peers = jnp.where(
+        head, 2 + 3 * low_n + 2 * top_n + far_n, usual + relay.astype(jnp.int32)
+        + 2 * jnp.logical_and(tail, d == 0).astype(jnp.int32),
+    )
 
     loads = []
 
@@ -224,52 +265,125 @@
             nd[k % 4, DISP[1] + k // 4, c * 5 : c * 5 + 4, :] = y[k * 8 + 4 : k * 8 + 8, lanes]
     for a in range(4):
         for k in range(3):
-            hy1[a * 12 + k * 4 : a * 12 + k * 4 + 4, :] = nd[a, k, pl.ds(0, 4, stride=5), :]
+            row = a * 12 + k * 4
+            hy0[row : row + 4, :] = nd[a, k, pl.ds(0, 4, stride=5), :]
+            hy1[row : row + 4, :] = nd[a, 3 + k, pl.ds(0, 4, stride=5), :]
 
     pl.semaphore_wait(barrier, peers)
+
+    @pl.when(tail)
+    def _():
+        def announce(*target):
+            pl.semaphore_signal(ready, inc=1, device_id=target, device_id_type=MESH)
+
+        announce(sp, d)
+
+        @pl.when(has_low)
+        def _():
+            announce(sp, dm)
+
+        @pl.when(has_top)
+        def _():
+            announce(sp, dp)
+
+        @pl.when(d == 0)
+        def _():
+            for k in (2, 3):
+                announce(sp, k)
 
     def remote(src, dst, send, recv, target):
         return pltpu.make_async_remote_copy(
             src_ref=src, dst_ref=dst, send_sem=send, recv_sem=recv, device_id=target, device_id_type=MESH
         )
 
-    def halo(first, slots, rows, recv_rows, corner):
-        h = 0 if first else 3
+    groups = [
+        (slice(0, 3), hy0, ry0, rc0, rl0),
+        (slice(3, 6), hy1, ry1, rc1, rl1),
+        (slice(6, 13), hy2, ry2, rc2, rl2),
+    ]
+
+    def halo(g):
+        slots, rows, recv_rows, corner, relay_corner = groups[g]
         size = corner.shape[0]
-        low = [
-            remote(rows.at[0:size], corner, h_send.at[h + 2], h_recv.at[h + 2], (sm, dm)),
-            remote(rows, recv_rows, h_send.at[h], h_recv.at[h], (s, dm)),
-        ]
-        side = remote(nd.at[0, slots], nd.at[4, slots], h_send.at[h + 1], h_recv.at[h + 1], (sm, d))
-        return low, side
-
-    def halo_start(*args):
-        low, side = halo(*args)
+        side_src, corner_src = nd.at[0, slots], rows.at[0:size]
+        below = remote(rows, recv_rows, h_send.at[g, 0], h_recv.at[g, 0], (s, dm))
+        side = remote(side_src, nd.at[4, slots], h_send.at[g, 1], h_recv.at[g, 1], (sm, d))
+        edge = remote(corner_src, corner, h_send.at[g, 2], h_recv.at[g, 2], (sm, dm))
+        to_relay = (
+            remote(side_src, rlp.at[slots], h_send.at[g, 1], l_recv.at[g, 0], (row_before, d)),
+            remote(corner_src, relay_corner, h_send.at[g, 2], l_recv.at[g, 1], (row_before, dm)),
+        )
+        end = s + (ROW - 2)
+        from_relay = (
+            remote(rlp.at[slots], nd.at[4, slots], l_send.at[g, 0], h_recv.at[g, 1], (end, d)),
+            remote(relay_corner, corner, l_send.at[g, 1], h_recv.at[g, 2], (end, d)),
+        )
+        return below, side, edge, to_relay, from_relay
+
+    def halo_start(g):
+        below, side, edge, to_relay, _ = halo(g)
+
+        @pl.when(head)
+        def _():
+            to_relay[0].start()
+
+            @pl.when(has_low)
+            def _():
+                to_relay[1].start()
+
+        @pl.when(not_head)
+        def _():
+            side.start()
+
+            @pl.when(has_low)
+            def _():
+                edge.start()
 
         @pl.when(has_low)
         def _():
-            for copy in low:
-                copy.start()
-
-        side.start()
-
-    def halo_wait(*args):
-        low, side = halo(*args)
+            below.start()
+
+    def forward(gs):
+        @pl.when(relay)
+        def _():
+            for g in gs:
+                _, _, _, to_relay, from_relay = halo(g)
+                to_relay[0].wait_recv()
+                from_relay[0].start()
+
+                @pl.when(has_top)
+                def _():
+                    to_relay[1].wait_recv()
+                    from_relay[1].start()
+
+    def forward_wait(gs):
+        @pl.when(relay)
+        def _():
+            for g in gs:
+                from_relay = halo(g)[4]
+                from_relay[0].wait_send()
+
+                @pl.when(has_top)
+                def _():
+                    from_relay[1].wait_send()
+
+    def halo_wait(g):
+        below, side, edge, _, _ = halo(g)
         side.wait()
 
         @pl.when(has_low)
         def _():
-            for copy in low:
-                copy.wait_send()
+            below.wait_send()
+            edge.wait_send()
 
         @pl.when(has_top)
         def _():
-            for copy in low:
-                copy.wait_recv()
-
-    h1 = (True, slice(0, 3), hy1, ry1, rc1)
-    h2 = (False, slice(3, 13), hy2, ry2, rc2)
-    halo_start(*h1)
+            below.wait_recv()
+            edge.wait_recv()
+
+    halo_start(0)
+    halo_start(1)
+    forward((0, 1))
 
     l_vg.wait()
     l_vc.wait()
@@ -285,14 +399,14 @@
         for c in range(4):
             nd[k, RHO, c * 5 : c * 5 + 4, :] = y[k * 8 : k * 8 + 4, c * 128 : c * 128 + 128]
     for a in range(4):
-        for k in range(10):
-            row = a * 40 + k * 4
-            hy2[row : row + 4, :] = nd[a, 3 + k, pl.ds(0, 4, stride=5), :]
-    halo_start(*h2)
+        for k in range(7):
+            row = a * 28 + k * 4
+            hy2[row : row + 4, :] = nd[a, 6 + k, pl.ds(0, 4, stride=5), :]
+    halo_start(2)
 
     @pl.when(d == nd_ - 1)
     def _():
-        for ref in (ry1, ry2, rc1, rc2):
+        for ref in (ry0, ry1, ry2, rc0, rc1, rc2):
             ref[...] = jnp.ones(ref.shape, F32)
         for n in range(2 * STEPS):
             rym[n] = jnp.zeros((64, 128), F32)
@@ -344,7 +458,9 @@
             )
             fg_own[x * 8 + 4 + t : x * 8 + 5 + t, :] = g[63 - t : 64 - t]
     far = remote(fg_own.at[0:8], fgb.at[d, 32:40], g_send.at[0], g_recv.at[4 + d], (sm, 0))
-    far.start()
+    @pl.when(not_head)
+    def _():
+        far.start()
 
     @pl.when(d != 0)
     def _():
@@ -436,16 +552,24 @@
 
         @pl.when(has_low)
         def _():
-            for copy in low:
+            for copy in low[:2]:
                 copy.start()
 
         @pl.when(has_top)
         def _():
-            for copy in top:
+            for copy in top[:2]:
                 copy.start()
 
         for copy in side:
             copy.start()
+
+        @pl.when(has_low)
+        def _():
+            low[2].start()
+
+        @pl.when(has_top)
+        def _():
+            top[2].start()
 
     def wait_all(w, t, name):
         low, top, side = messages(w, t)
@@ -538,32 +662,41 @@
             f = f + fgn[(4 + m) * 24 : (5 + m) * 24, :] * sj[t - m]
         frc[...] = f
 
-    halo_wait(*h1)
-    for a in range(4):
-        for k in range(3):
-            row = a * 12 + k * 4
-            nd[a, k, pl.ds(4, 4, stride=5), :] = below * ry1[row : row + 4, :]
-    for k in range(3):
-        nd[4, k, pl.ds(4, 4, stride=5), :] = below * rc1[k * 4 : k * 4 + 4, :]
+    def fill(g, count):
+        slots, _, recv_rows, corner, _ = groups[g]
+        first = slots.start
+        for a in range(5):
+            for k in range(count):
+                row = (a * count + k) * 4
+                top = corner[k * 4 : k * 4 + 4, :] if a == 4 else recv_rows[row : row + 4, :]
+                nd[a, first + k, pl.ds(4, 4, stride=5), :] = top if first + k == RHO else below * top
+
+    halo_wait(0)
+    fill(0, 3)
     l_opg.wait()
     l_opf.wait()
     strain_stress_force(0, 0)
+
+    @pl.when(head)
+    def _():
+        pl.semaphore_wait(ready, 1 + low_n + top_n + far_n)
+
     send(0, 0)
 
+    @pl.when(head)
+    def _():
+        far.start()
+
+    forward((2,))
     l_rc.wait()
     relaxed(1)
-    halo_wait(*h2)
-    for a in range(4):
-        for k in range(10):
-            row = a * 40 + k * 4
-            top = ry2[row : row + 4, :]
-            nd[a, 3 + k, pl.ds(4, 4, stride=5), :] = top if k == 9 else below * top
-    for k in range(10):
-        top = rc2[k * 4 : k * 4 + 4, :]
-        nd[4, 3 + k, pl.ds(4, 4, stride=5), :] = top if k == 9 else below * top
+    halo_wait(1)
+    fill(1, 3)
     strain_stress_force(1, 0)
     send(1, 0)
     memory(0, False)
+    halo_wait(2)
+    fill(2, 7)
     first = (d == 0).astype(F32)
     row_factor = tab_v[1, 0:24] * (1.0 + first * tab_v[2, 0:24] - (1.0 - below) * tab_v[3, 0:24])
     for a in range(5):
@@ -609,11 +742,12 @@
     for t in range(STEPS):
         receive(0, t)
         update(0)
+        if t < STEPS - 1:
+            strain_stress_force(0, t + 1)
+            send(0, t + 1)
         sample(t)
         forcing(t)
         if t < STEPS - 1:
-            strain_stress_force(0, t + 1)
-            send(0, t + 1)
             if t > 0:
                 memory(1, False)
         else:
@@ -627,6 +761,7 @@
             memory(0, t == STEPS - 2)
         else:
             finish(1)
+    forward_wait((0, 1, 2))
     for w in range(2):
         for t in range(STEPS):
             wait_all(w, t, "wait_send")
@@ -684,11 +819,13 @@
             vm(waves, 64, 128), vm(waves, 64, 128),
             vm(waves, 3, 24, 128), vm(waves, 3, 24, 128),
             vm(waves, 64, 128), vm(waves, 64, 128), vm(waves, 4, 16, 128),
-            vm(48, 128), vm(160, 128), vm(48, 128), vm(160, 128), vm(16, 128), vm(40, 128),
+            vm(48, 128), vm(48, 128), vm(112, 128), vm(48, 128), vm(48, 128), vm(112, 128),
+            vm(16, 128), vm(16, 128), vm(32, 128), vm(SLOTS, 24, 128), vm(16, 128), vm(16, 128), vm(32, 128),
             vm(4, 72, 128), pltpu.VMEM((4, 128), jnp.int32), vm(64, 256),
             vm(32, 128), vm(4, 40, 128), vm(192, 128), vm(STEPS, 24, 128), vm(24, 128),
             vm(4, 96, 128),
-            pltpu.SMEM((3,), F32), dma((24,)), dma((6,)), dma((6,)), dma((waves, 8)), dma((waves, 8)),
+            pltpu.SMEM((3,), F32), dma((24,)), pltpu.SemaphoreType.REGULAR,
+            dma((3, 3)), dma((3, 3)), dma((3, 2)), dma((3, 2)), dma((waves, 8)), dma((waves, 8)),
             dma((2,)), dma((8,)),
         ],
         compiler_params=pltpu.CompilerParams(

time: 38.2 us -> 36.5 us (0.955)
  the two profiles are of different devices: /device:TPU:1 before, /device:TPU:0 now
where the time goes in v4:
time: 36.5 us; the launch traced here: 36.4 us
  Pallas kernels  35.8 us (98%)
  between operations  0.65 us (2%)
    pallas_call x1, Pallas kernels, body(): pl.pallas_call(kernel, out_shape=(vm(2, 75, 32, 128), vm(2, 12, 8, 512)),...  34.3 us
    pallas_call x1, Pallas kernels, body(): pl.pallas_call(write_kernel, out_shape=(nodal, nodal, points, nodal, noda...  1.42 us

profile of v4, /device:TPU:0, one launch (start us, length us, event | category | flops | bytes accessed | tf_op | source)
XLA Modules:
  0.0 36.4 jit_solution(2703453872740915383)
XLA Ops:
  0.6 34.3 %shard_map.217 = (f32[2,75,32,128]{3,2,1,0:T(8,128)S(1)}, f32[2,12,8,512]{3,2,1,0:T(8,128)S(1)}) custom-call(f32[12,4,512]{2,1,0:T(4,128)} %bitcast.22, f32[12,4,512]{2,1,0:T(4,128)} %bitcast.23, f32[75,25,1,128]{3,2,1,0:T(1,128)} %bitcast.20, f32[12,4,512]{2,1,0:T(4,128)} %bitcast.24, f32[12,4,512]{2,1,0:T(4,128)} %bitcast.25, f32[75,25,1,128]{3,2,1,0:T(1,128)} %bitcast.21, ...), custom_call_target="tpu_custom_call" | custom-call | tf_op jit(solution)/shard_map/pallas_call | solution.py:807
  35.0 1.4 %shard_map.218 = (f32[12,4,512]{2,1,0:T(4,128)}, f32[12,4,512]{2,1,0:T(4,128)}, f32[75,25,1,128]{3,2,1,0:T(1,128)}, f32[12,4,512]{2,1,0:T(4,128)}, f32[12,4,512]{2,1,0:T(4,128)}, /*index=5*/f32[75,25,1,128]{3,2,1,0:T(1,128)}) custom-call(f32[2,75,32,128]{3,2,1,0:T(8,128)S(1)} %get-tuple-element.14.mem, f32[2,12,8,512]{3,2,1,0:T(8,128)S(1)} %get-tuple-element.15.out_v), custom_call_target="tpu_custom_call" | custom-call | tf_op jit(solution)/shard_map/pallas_call | solution.py:835

commit v5 on v4

--- a/solution.py
+++ b/solution.py
@@ -241,6 +241,28 @@
     l_hist = [load(hist.at[:, x], hist_v.at[x, 0:64]) for x in range(4)]
     l_rc = load(rc.at[:, :, 0], mem.at[1, :, 0:25])
 
+    @pl.when(tail)
+    def _():
+        pl.semaphore_wait(barrier, peers)
+
+        def announce(*target):
+            pl.semaphore_signal(ready, inc=1, device_id=target, device_id_type=MESH)
+
+        announce(sp, d)
+
+        @pl.when(has_low)
+        def _():
+            announce(sp, dm)
+
+        @pl.when(has_top)
+        def _():
+            announce(sp, dp)
+
+        @pl.when(d == 0)
+        def _():
+            for k in (2, 3):
+                announce(sp, k)
+
     zero24 = jnp.zeros((24, 128), F32)
     for a in range(4):
         for k in range(SLOTS):
@@ -269,27 +291,9 @@
             hy0[row : row + 4, :] = nd[a, k, pl.ds(0, 4, stride=5), :]
             hy1[row : row + 4, :] = nd[a, 3 + k, pl.ds(0, 4, stride=5), :]
 
-    pl.semaphore_wait(barrier, peers)
-
-    @pl.when(tail)
-    def _():
-        def announce(*target):
-            pl.semaphore_signal(ready, inc=1, device_id=target, device_id_type=MESH)
-
-        announce(sp, d)
-
-        @pl.when(has_low)
-        def _():
-            announce(sp, dm)
-
-        @pl.when(has_top)
-        def _():
-            announce(sp, dp)
-
-        @pl.when(d == 0)
-        def _():
-            for k in (2, 3):
-                announce(sp, k)
+    @pl.when(not_tail)
+    def _():
+        pl.semaphore_wait(barrier, peers)
 
     def remote(src, dst, send, recv, target):
         return pltpu.make_async_remote_copy(
@@ -680,12 +684,9 @@
     @pl.when(head)
     def _():
         pl.semaphore_wait(ready, 1 + low_n + top_n + far_n)
+        far.start()
 
     send(0, 0)
-
-    @pl.when(head)
-    def _():
-        far.start()
 
     forward((2,))
     l_rc.wait()
@@ -703,26 +704,6 @@
         wx = float([0.2, 49.0 / 90.0, 32.0 / 45.0, 49.0 / 90.0, 0.2][a])
         inv_mass[a] = (DT / wx) * row_factor / (nd[a, RHO] + tab_v[4, 0:24])
 
-    @pl.when(d == 0)
-    def _():
-        for j in range(1, 4):
-            remote(fg_own, fgb.at[j, 0:32], g_send.at[1], g_recv.at[j], (s, 0)).wait_recv()
-        for j in range(4):
-            remote(fg_own.at[0:8], fgb.at[j, 32:40], g_send.at[0], g_recv.at[4 + j], (sm, 0)).wait_recv()
-        fgb[0, 0:32, :] = fg_own[...]
-        x = jnp.concatenate([fgb[j] for j in range(4)], axis=1)
-        y = jnp.dot(jnp.concatenate(split3(x), axis=0), perm_v[...], preferred_element_type=F32)
-        y = y[0:40] + y[40:80] + y[80:120]
-        for a in range(5):
-            for c in range(4):
-                fgn[pl.ds(a * 4 + c, 8, stride=24), :] = y[a * 8 : a * 8 + 8, c * 128 : c * 128 + 128]
-
-    far.wait_send()
-
-    @pl.when(d != 0)
-    def _():
-        remote(fg_own, fgb.at[d, 0:32], g_send.at[1], g_recv.at[d], (s, 0)).wait_send()
-
     memory(1, False)
 
     def finish(w):
@@ -739,6 +720,19 @@
         )
         out_v[w] = (y[0:96] + y[96:192] + y[192:288]).reshape(12, 8, 512)
 
+    def gather():
+        for j in range(1, 4):
+            remote(fg_own, fgb.at[j, 0:32], g_send.at[1], g_recv.at[j], (s, 0)).wait_recv()
+        for j in range(4):
+            remote(fg_own.at[0:8], fgb.at[j, 32:40], g_send.at[0], g_recv.at[4 + j], (sm, 0)).wait_recv()
+        fgb[0, 0:32, :] = fg_own[...]
+        x = jnp.concatenate([fgb[j] for j in range(4)], axis=1)
+        y = jnp.dot(jnp.concatenate(split3(x), axis=0), perm_v[...], preferred_element_type=F32)
+        y = y[0:40] + y[40:80] + y[80:120]
+        for a in range(5):
+            for c in range(4):
+                fgn[pl.ds(a * 4 + c, 8, stride=24), :] = y[a * 8 : a * 8 + 8, c * 128 : c * 128 + 128]
+
     for t in range(STEPS):
         receive(0, t)
         update(0)
@@ -746,6 +740,8 @@
             strain_stress_force(0, t + 1)
             send(0, t + 1)
         sample(t)
+        if t == 0:
+            pl.when(d == 0)(gather)
         forcing(t)
         if t < STEPS - 1:
             if t > 0:
@@ -762,6 +758,11 @@
         else:
             finish(1)
     forward_wait((0, 1, 2))
+    far.wait_send()
+
+    @pl.when(d != 0)
+    def _():
+        remote(fg_own, fgb.at[d, 0:32], g_send.at[1], g_recv.at[d], (s, 0)).wait_send()
     for w in range(2):
         for t in range(STEPS):
             wait_all(w, t, "wait_send")

time: 36.5 us -> 35.7 us (0.978)
  the two profiles are of different devices: /device:TPU:0 before, /device:TPU:1 now
where the time goes in v5:
time: 35.7 us; the launch traced here: 35.6 us
  Pallas kernels  34.9 us (98%)
  between operations  0.65 us (2%)
    pallas_call x1, Pallas kernels, body(): pl.pallas_call(kernel, out_shape=(vm(2, 75, 32, 128), vm(2, 12, 8, 512)),...  33.5 us
    pallas_call x1, Pallas kernels, body(): pl.pallas_call(write_kernel, out_shape=(nodal, nodal, points, nodal, noda...  1.42 us

profile of v5, /device:TPU:1, one launch (start us, length us, event | category | flops | bytes accessed | tf_op | source)
XLA Modules:
  0.0 35.6 jit_solution(8255177839176916522)
XLA Ops:
  0.6 33.5 %shard_map.217 = (f32[2,75,32,128]{3,2,1,0:T(8,128)S(1)}, f32[2,12,8,512]{3,2,1,0:T(8,128)S(1)}) custom-call(f32[12,4,512]{2,1,0:T(4,128)} %bitcast.22, f32[12,4,512]{2,1,0:T(4,128)} %bitcast.23, f32[75,25,1,128]{3,2,1,0:T(1,128)} %bitcast.20, f32[12,4,512]{2,1,0:T(4,128)} %bitcast.24, f32[12,4,512]{2,1,0:T(4,128)} %bitcast.25, f32[75,25,1,128]{3,2,1,0:T(1,128)} %bitcast.21, ...), custom_call_target="tpu_custom_call" | custom-call | tf_op jit(solution)/shard_map/pallas_call | solution.py:808
  34.1 1.4 %shard_map.218 = (f32[12,4,512]{2,1,0:T(4,128)}, f32[12,4,512]{2,1,0:T(4,128)}, f32[75,25,1,128]{3,2,1,0:T(1,128)}, f32[12,4,512]{2,1,0:T(4,128)}, f32[12,4,512]{2,1,0:T(4,128)}, /*index=5*/f32[75,25,1,128]{3,2,1,0:T(1,128)}) custom-call(f32[2,75,32,128]{3,2,1,0:T(8,128)S(1)} %get-tuple-element.14.mem, f32[2,12,8,512]{3,2,1,0:T(8,128)S(1)} %get-tuple-element.15.out_v), custom_call_target="tpu_custom_call" | custom-call | tf_op jit(solution)/shard_map/pallas_call | solution.py:836

commit v6 on v5

--- a/solution.py
+++ b/solution.py
@@ -124,11 +124,11 @@
     mem, out_v,
     pair_u, pair_v, pair_r, perm_v, opg_v, opf_v, tab_v,
     sw, qs, lam_v, mu_v, def_v, inv_mass,
-    nd, ft, fs, yp, ym, rxm, rxp, rym, ryp, rdg,
-    hy0, hy1, hy2, ry0, ry1, ry2, rc0, rc1, rc2, rlp, rl0, rl1, rl2,
+    nd, ft, fs, cr, yp, ym, rxm, rxp, rym, ryp, rdg,
+    hy0, hy1, hy2, ry0, ry1, ry2, rc0, rc1, rc2, rlp, rl0, rl1, rl2, rlf,
     hist_v, cells_v, filt_v, fg_own, fgb, fgn, sj, frc,
     xr,
-    keep_s, lsem, ready, h_send, h_recv, l_send, l_recv, f_send, f_recv, g_send, g_recv,
+    keep_s, lsem, ready, r_send, r_recv, h_send, h_recv, l_send, l_recv, f_send, f_recv, g_send, g_recv,
 ):
     s = lax.axis_index("slab")
     d = lax.axis_index("depth")
@@ -160,9 +160,10 @@
     def _():
         greet(s - (ROW - 2), d)
 
-    @pl.when(jnp.logical_and(head, d >= 2))
-    def _():
-        greet(sm, 0)
+        @pl.when(d == 0)
+        def _():
+            for k in (1, 2, 3):
+                greet(s - (ROW - 2), k)
 
     @pl.when(not_tail)
     def _():
@@ -200,8 +201,9 @@
     low_n, top_n, far_n = (flag.astype(jnp.int32) for flag in (has_low, has_top, d >= 2))
     usual = 2 + 3 * low_n + 3 * top_n + 2 * far_n
     peers = jnp.where(
-        head, 2 + 3 * low_n + 2 * top_n + far_n, usual + relay.astype(jnp.int32)
-        + 2 * jnp.logical_and(tail, d == 0).astype(jnp.int32),
+        head,
+        2 + 3 * low_n + 2 * top_n + far_n,
+        usual + relay.astype(jnp.int32) * (1 + low_n),
     )
 
     loads = []
@@ -258,11 +260,6 @@
         def _():
             announce(sp, dp)
 
-        @pl.when(d == 0)
-        def _():
-            for k in (2, 3):
-                announce(sp, k)
-
     zero24 = jnp.zeros((24, 128), F32)
     for a in range(4):
         for k in range(SLOTS):
@@ -462,15 +459,22 @@
             )
             fg_own[x * 8 + 4 + t : x * 8 + 5 + t, :] = g[63 - t : 64 - t]
     far = remote(fg_own.at[0:8], fgb.at[d, 32:40], g_send.at[0], g_recv.at[4 + d], (sm, 0))
+    far_to_relay = remote(fg_own.at[0:8], rlf, g_send.at[0], r_recv.at[0], (row_before, d))
+    far_from_relay = remote(rlf, fgb.at[d, 32:40], r_send.at[0], g_recv.at[4 + d], (s + (ROW - 2), 0))
+
     @pl.when(not_head)
     def _():
         far.start()
 
+    @pl.when(head)
+    def _():
+        far_to_relay.start()
+
     @pl.when(d != 0)
     def _():
         remote(fg_own, fgb.at[d, 0:32], g_send.at[1], g_recv.at[d], (s, 0)).start()
 
-    def strain_stress_force(w, t):
+    def strain_stress(w, t):
         opg_m = opg_v[...]
         comps = []
         for i in range(3):
@@ -506,40 +510,45 @@
             sxz = m * xz - r[3]
             syz = m * yz - r[4]
             fluxes.append(((sxx, sxy, sxz), (sxy, syy, syz), (sxz, syz, szz)))
-        opf_m = opf_v[...]
-        for i in range(3):
-            fx = derive([fluxes[a][0][i] for a in range(5)], DMAT.T)
+        flux_x = [derive([fluxes[a][0][i] for a in range(5)], DMAT.T) for i in range(3)]
+
+        def force(planes):
             columns = []
-            for a in range(5):
-                y_high, y_low = split2(fluxes[a][1][i])
-                z_high, z_low = split2(fluxes[a][2][i])
-                x_high, x_low = split2(fx[a])
-                columns.append(
-                    jnp.concatenate([y_high, z_high, y_low, z_low, y_high, z_high, x_high, x_low], axis=0)
-                )
-            f = jnp.dot(opf_m, jnp.concatenate(columns, axis=1), preferred_element_type=F32)
-            for a in range(5):
-                fa = f[:, a * 128 : a * 128 + 128]
-                fs[w, t, a, i, 0:8, :] = fa[0:8] + pltpu.roll(fa[24:32], 1, 1)
-                fs[w, t, a, i, 8:24, :] = fa[8:24]
+            for a in planes:
+                for i in range(3):
+                    y_high, y_low = split2(fluxes[a][1][i])
+                    z_high, z_low = split2(fluxes[a][2][i])
+                    x_high, x_low = split2(flux_x[i][a])
+                    columns.append(
+                        jnp.concatenate([y_high, z_high, y_low, z_low, y_high, z_high, x_high, x_low], axis=0)
+                    )
+            f = jnp.dot(opf_v[...], jnp.concatenate(columns, axis=1), preferred_element_type=F32)
+            for k, a in enumerate(planes):
+                for i in range(3):
+                    lane = (k * 3 + i) * 128
+                    fa = f[:, lane : lane + 128]
+                    fs[w, t, a, i, 0:8, :] = fa[0:8] + pltpu.roll(fa[24:32], 1, 1)
+                    fs[w, t, a, i, 8:24, :] = fa[8:24]
+
+        return force
 
     below = (d < nd_ - 1).astype(F32)
 
     def messages(w, t):
         n = w * STEPS + t
         low = [
-            (ym.at[n, 0:16], rdg.at[n, 0], (sm, dm)),
-            (ym.at[n, 48:64], rdg.at[n, 2], (sp, dm)),
-            (ym.at[n], rym.at[n], (s, dm)),
+            (cr.at[n, 0, 0:12], rdg.at[n, 0, 0:12], (sm, dm)),
+            (cr.at[n, 2, 0:12], rdg.at[n, 2, 0:12], (sp, dm)),
+            (ym.at[n, 0:60], rym.at[n, 0:60], (s, dm)),
         ]
         top = [
-            (yp.at[n, 0:16], rdg.at[n, 1], (sm, dp)),
-            (yp.at[n, 48:64], rdg.at[n, 3], (sp, dp)),
-            (yp.at[n], ryp.at[n], (s, dp)),
+            (cr.at[n, 1, 0:12], rdg.at[n, 1, 0:12], (sm, dp)),
+            (cr.at[n, 3, 0:12], rdg.at[n, 3, 0:12], (sp, dp)),
+            (yp.at[n, 0:60], ryp.at[n, 0:60], (s, dp)),
         ]
         side = [
-            (fs.at[w, t, 0], rxm.at[n], (sm, d)),
-            (fs.at[w, t, 4], rxp.at[n], (sp, d)),
+            (fs.at[w, t, 0, :, 0:20], rxm.at[n, :, 0:20], (sm, d)),
+            (fs.at[w, t, 4, :, 0:20], rxp.at[n, :, 0:20], (sp, d)),
         ]
         made = []
         for base, group in ((0, low), (3, top), (6, side)):
@@ -551,7 +560,7 @@
             )
         return made
 
-    def start_all(w, t):
+    def start_outer(w, t):
         low, top, side = messages(w, t)
 
         @pl.when(has_low)
@@ -566,6 +575,9 @@
 
         for copy in side:
             copy.start()
+
+    def start_inner(w, t):
+        low, top, _ = messages(w, t)
 
         @pl.when(has_low)
         def _():
@@ -591,16 +603,24 @@
             for copy in top:
                 getattr(copy, name)()
 
-    def send(w, t):
+    def step(w, t, gate=None):
         n = w * STEPS + t
+        force = strain_stress(w, t)
+        force((0, 4))
+        for k, a in enumerate((0, 4)):
+            for i in range(3):
+                for b in range(2):
+                    cr[n, 2 * k + b, i * 4 : i * 4 + 4, :] = fs[w, t, a, i, pl.ds(4 * b, 4, stride=5), :]
+        if gate is not None:
+            gate()
+        start_outer(w, t)
+        force((1, 2, 3))
         for a in range(5):
             for i in range(3):
                 row = a * 12 + i * 4
                 ym[n, row : row + 4, :] = fs[w, t, a, i, pl.ds(0, 4, stride=5), :]
                 yp[n, row : row + 4, :] = fs[w, t, a, i, pl.ds(4, 4, stride=5), :]
-        ym[n, 60:64, :] = jnp.zeros((4, 128), F32)
-        yp[n, 60:64, :] = jnp.zeros((4, 128), F32)
-        start_all(w, t)
+        start_inner(w, t)
 
     l_keep.wait()
     kept = [keep_s[l] for l in range(3)]
@@ -679,22 +699,26 @@
     fill(0, 3)
     l_opg.wait()
     l_opf.wait()
-    strain_stress_force(0, 0)
-
-    @pl.when(head)
-    def _():
-        pl.semaphore_wait(ready, 1 + low_n + top_n + far_n)
-        far.start()
-
-    send(0, 0)
+
+    def gate():
+        @pl.when(head)
+        def _():
+            pl.semaphore_wait(ready, 1 + low_n + top_n)
+
+    step(0, 0, gate)
 
     forward((2,))
+
+    @pl.when(relay)
+    def _():
+        far_to_relay.wait_recv()
+        far_from_relay.start()
+
     l_rc.wait()
     relaxed(1)
     halo_wait(1)
     fill(1, 3)
-    strain_stress_force(1, 0)
-    send(1, 0)
+    step(1, 0)
     memory(0, False)
     halo_wait(2)
     fill(2, 7)
@@ -737,8 +761,7 @@
         receive(0, t)
         update(0)
         if t < STEPS - 1:
-            strain_stress_force(0, t + 1)
-            send(0, t + 1)
+            step(0, t + 1)
         sample(t)
         if t == 0:
             pl.when(d == 0)(gather)
@@ -752,12 +775,16 @@
         receive(1, t)
         update(1)
         if t < STEPS - 1:
-            strain_stress_force(1, t + 1)
-            send(1, t + 1)
+            step(1, t + 1)
             memory(0, t == STEPS - 2)
         else:
             finish(1)
     forward_wait((0, 1, 2))
+
+    @pl.when(relay)
+    def _():
+        far_from_relay.wait_send()
+
     far.wait_send()
 
     @pl.when(d != 0)
@@ -817,15 +844,17 @@
             vm(2, 25, 32, 128), vm(2, 25, 32, 128),
             vm(5, 32, 128), vm(5, 32, 128), vm(5, 32, 128), vm(5, 24, 128),
             vm(5, SLOTS, 24, 128), vm(5, 3, 24, 128), vm(2, STEPS, 5, 3, 24, 128),
+            vm(waves, 4, 16, 128),
             vm(waves, 64, 128), vm(waves, 64, 128),
             vm(waves, 3, 24, 128), vm(waves, 3, 24, 128),
             vm(waves, 64, 128), vm(waves, 64, 128), vm(waves, 4, 16, 128),
             vm(48, 128), vm(48, 128), vm(112, 128), vm(48, 128), vm(48, 128), vm(112, 128),
             vm(16, 128), vm(16, 128), vm(32, 128), vm(SLOTS, 24, 128), vm(16, 128), vm(16, 128), vm(32, 128),
+            vm(8, 128),
             vm(4, 72, 128), pltpu.VMEM((4, 128), jnp.int32), vm(64, 256),
             vm(32, 128), vm(4, 40, 128), vm(192, 128), vm(STEPS, 24, 128), vm(24, 128),
             vm(4, 96, 128),
-            pltpu.SMEM((3,), F32), dma((24,)), pltpu.SemaphoreType.REGULAR,
+            pltpu.SMEM((3,), F32), dma((24,)), pltpu.SemaphoreType.REGULAR, dma((1,)), dma((1,)),
             dma((3, 3)), dma((3, 3)), dma((3, 2)), dma((3, 2)), dma((waves, 8)), dma((waves, 8)),
             dma((2,)), dma((8,)),
         ],

time: 35.7 us -> 35.3 us (0.989)
  no operation moved by 1% of the time
where the time goes in v6:
time: 35.3 us; the launch traced here: 35.2 us
  Pallas kernels  34.6 us (98%)
  between operations  0.65 us (2%)
    pallas_call x1, Pallas kernels, body(): pl.pallas_call(kernel, out_shape=(vm(2, 75, 32, 128), vm(2, 12, 8, 512)),...  33.1 us
    pallas_call x1, Pallas kernels, body(): pl.pallas_call(write_kernel, out_shape=(nodal, nodal, points, nodal, noda...  1.42 us

profile of v6, /device:TPU:1, one launch (start us, length us, event | category | flops | bytes accessed | tf_op | source)
XLA Modules:
  0.0 35.2 jit_solution(17688859640385758464)
XLA Ops:
  0.6 33.1 %shard_map.217 = (f32[2,75,32,128]{3,2,1,0:T(8,128)S(1)}, f32[2,12,8,512]{3,2,1,0:T(8,128)S(1)}) custom-call(f32[12,4,512]{2,1,0:T(4,128)} %bitcast.22, f32[12,4,512]{2,1,0:T(4,128)} %bitcast.23, f32[75,25,1,128]{3,2,1,0:T(1,128)} %bitcast.20, f32[12,4,512]{2,1,0:T(4,128)} %bitcast.24, f32[12,4,512]{2,1,0:T(4,128)} %bitcast.25, f32[75,25,1,128]{3,2,1,0:T(1,128)} %bitcast.21, ...), custom_call_target="tpu_custom_call" | custom-call | tf_op jit(solution)/shard_map/pallas_call | solution.py:835
  33.8 1.4 %shard_map.218 = (f32[12,4,512]{2,1,0:T(4,128)}, f32[12,4,512]{2,1,0:T(4,128)}, f32[75,25,1,128]{3,2,1,0:T(1,128)}, f32[12,4,512]{2,1,0:T(4,128)}, f32[12,4,512]{2,1,0:T(4,128)}, /*index=5*/f32[75,25,1,128]{3,2,1,0:T(1,128)}) custom-call(f32[2,75,32,128]{3,2,1,0:T(8,128)S(1)} %get-tuple-element.14.mem, f32[2,12,8,512]{3,2,1,0:T(8,128)S(1)} %get-tuple-element.15.out_v), custom_call_target="tpu_custom_call" | custom-call | tf_op jit(solution)/shard_map/pallas_call | solution.py:865

commit v7 on v6

--- a/solution.py
+++ b/solution.py
@@ -119,15 +119,22 @@
     return out
 
 
+def to_nodes(xr, perm):
+    x = jnp.concatenate([xr[c] for c in range(4)], axis=1)
+    y = lax.dot_general(
+        jnp.concatenate(split3(x), axis=0), perm[...], (((1,), (1,)), ((), ())), preferred_element_type=F32
+    )
+    return (y[0:96] + y[96:192] + y[192:288]).reshape(12, 8, 512)
+
+
 def kernel(
     ug, vg, rg, uc, vc, rc, lam, mu, defect, keep, rho, hist, cells, filt, perm, opg, opf, table,
-    mem, out_v,
-    pair_u, pair_v, pair_r, perm_v, opg_v, opf_v, tab_v,
+    mem, out_v, xr, perm_v,
+    pair_u, pair_v, pair_r, opg_v, opf_v, tab_v,
     sw, qs, lam_v, mu_v, def_v, inv_mass,
     nd, ft, fs, cr, yp, ym, rxm, rxp, rym, ryp, rdg,
     hy0, hy1, hy2, ry0, ry1, ry2, rc0, rc1, rc2, rlp, rl0, rl1, rl2, rlf,
     hist_v, cells_v, filt_v, fg_own, fgb, fgn, sj, frc,
-    xr,
     keep_s, lsem, ready, r_send, r_recv, h_send, h_recv, l_send, l_recv, f_send, f_recv, g_send, g_recv,
 ):
     s = lax.axis_index("slab")
@@ -737,12 +744,8 @@
                 for c in range(4):
                     xr[c, row : row + 4, :] = nd[x, DISP[w] + i, c * 5 : c * 5 + 4, :]
                     xr[c, row + 4 : row + 8, :] = nd[x, VEL[w] + i, c * 5 : c * 5 + 4, :]
-        x = jnp.concatenate([xr[c] for c in range(4)], axis=1)
-        y = lax.dot_general(
-            jnp.concatenate(split3(x), axis=0), perm_v[...], (((1,), (1,)), ((), ())),
-            preferred_element_type=F32,
-        )
-        out_v[w] = (y[0:96] + y[96:192] + y[192:288]).reshape(12, 8, 512)
+        if w == 0:
+            out_v[...] = to_nodes(xr, perm_v)
 
     def gather():
         for j in range(1, 4):
@@ -795,17 +798,20 @@
             wait_all(w, t, "wait_send")
 
 
-def write_kernel(mem, out_v, ug_o, vg_o, rg_o, uc_o, vc_o, rc_o, sem):
+def write_kernel(mem, out_v, xr, perm_v, ug_o, vg_o, rg_o, uc_o, vc_o, rc_o, last_v, sem):
     pairs = [
         (mem.at[0, :, 0:25], rg_o.at[:, :, 0]),
         (mem.at[1, :, 0:25], rc_o.at[:, :, 0]),
-        (out_v.at[0, :, 0:4], ug_o),
-        (out_v.at[0, :, 4:8], vg_o),
-        (out_v.at[1, :, 0:4], uc_o),
-        (out_v.at[1, :, 4:8], vc_o),
+        (out_v.at[:, 0:4], ug_o),
+        (out_v.at[:, 4:8], vg_o),
+        (last_v.at[:, 0:4], uc_o),
+        (last_v.at[:, 4:8], vc_o),
     ]
     copies = [pltpu.make_async_copy(src, dst, sem.at[j]) for j, (src, dst) in enumerate(pairs)]
-    for copy in copies:
+    for copy in copies[:4]:
+        copy.start()
+    last_v[...] = to_nodes(xr, perm_v)
+    for copy in copies[4:]:
         copy.start()
     for copy in copies:
         copy.wait()
@@ -834,12 +840,12 @@
     waves = 2 * STEPS
     results = pl.pallas_call(
         kernel,
-        out_shape=(vm(2, 75, 32, 128), vm(2, 12, 8, 512)),
+        out_shape=(vm(2, 75, 32, 128), vm(12, 8, 512), vm(4, 96, 128), pltpu.VMEM((512, 512), BF16)),
         in_specs=in_specs,
-        out_specs=(in_vmem,) * 2,
+        out_specs=(in_vmem,) * 4,
         scratch_shapes=[
             vm(12, 8, 512), vm(12, 8, 512), vm(4, 8, 512),
-            pltpu.VMEM((512, 512), BF16), pltpu.VMEM((96, 96), BF16), pltpu.VMEM((32, 256), BF16),
+            pltpu.VMEM((96, 96), BF16), pltpu.VMEM((32, 256), BF16),
             vm(5, 32, 128),
             vm(2, 25, 32, 128), vm(2, 25, 32, 128),
             vm(5, 32, 128), vm(5, 32, 128), vm(5, 32, 128), vm(5, 24, 128),
@@ -853,7 +859,6 @@
             vm(8, 128),
             vm(4, 72, 128), pltpu.VMEM((4, 128), jnp.int32), vm(64, 256),
             vm(32, 128), vm(4, 40, 128), vm(192, 128), vm(STEPS, 24, 128), vm(24, 128),
-            vm(4, 96, 128),
             pltpu.SMEM((3,), F32), dma((24,)), pltpu.SemaphoreType.REGULAR, dma((1,)), dma((1,)),
             dma((3, 3)), dma((3, 3)), dma((3, 2)), dma((3, 2)), dma((waves, 8)), dma((waves, 8)),
             dma((2,)), dma((8,)),
@@ -865,10 +870,10 @@
     outs = pl.pallas_call(
         write_kernel,
         out_shape=(nodal, nodal, points, nodal, nodal, points),
-        in_specs=(in_vmem,) * 2,
+        in_specs=(in_vmem,) * 4,
         out_specs=(in_hbm,) * 6,
-        scratch_shapes=[dma((6,))],
-        compiler_params=pltpu.CompilerParams(vmem_limit_bytes=1024 * 1024),
+        scratch_shapes=[vm(12, 8, 512), dma((6,))],
+        compiler_params=pltpu.CompilerParams(vmem_limit_bytes=8 * 1024 * 1024),
     )(*(pltpu.with_memory_space_constraint(x, pltpu.VMEM) for x in results))
     full = (3, 5, 5, 5, 5, 1, 1, 128)
     u = (3, 4, 4, 512)

time: 35.3 us -> 35 us (level)
  no operation moved by 1% of the time
where the time goes in v7:
time: 35 us; the launch traced here: 34.9 us
  Pallas kernels  34.3 us (98%)
  between operations  0.65 us (2%)
    pallas_call x1, Pallas kernels, body(): pl.pallas_call(kernel, out_shape=(vm(2, 75, 32, 128), vm(12, 8, 512), vm(...  32.8 us
    pallas_call x1, Pallas kernels, body(): pl.pallas_call(write_kernel, out_shape=(nodal, nodal, points, nodal, noda...  1.44 us

profile of v7, /device:TPU:1, one launch (start us, length us, event | category | flops | bytes accessed | tf_op | source)
XLA Modules:
  0.0 34.9 jit_solution(37588667991996208)
XLA Ops:
  0.6 32.8 %shard_map.217 = (f32[2,75,32,128]{3,2,1,0:T(8,128)S(1)}, f32[12,8,512]{2,1,0:T(8,128)S(1)}, f32[4,96,128]{2,1,0:T(8,128)S(1)}, bf16[512,512]{1,0:T(8,128)(2,1)S(1)}) custom-call(f32[12,4,512]{2,1,0:T(4,128)} %bitcast.22, f32[12,4,512]{2,1,0:T(4,128)} %bitcast.23, f32[75,25,1,128]{3,2,1,0:T(1,128)} %bitcast.20, f32[12,4,512]{2,1,0:T(4,128)} %bitcast.24, ...), custom_call_target="tpu_custom_call" | custom-call | tf_op jit(solution)/shard_map/pallas_call | solution.py:841
  33.5 1.4 %shard_map.218 = (f32[12,4,512]{2,1,0:T(4,128)}, f32[12,4,512]{2,1,0:T(4,128)}, f32[75,25,1,128]{3,2,1,0:T(1,128)}, f32[12,4,512]{2,1,0:T(4,128)}, f32[12,4,512]{2,1,0:T(4,128)}, /*index=5*/f32[75,25,1,128]{3,2,1,0:T(1,128)}) custom-call(f32[2,75,32,128]{3,2,1,0:T(8,128)S(1)} %get-tuple-element.16.mem, f32[12,8,512]{2,1,0:T(8,128)S(1)} %get-tuple-element.17.out_v, ...), custom_call_target="tpu_custom_call" | custom-call | tf_op jit(solution)/shard_map/pallas_call | solution.py:870
